TPU v7x, 256 devices: a whole 4x4x8 slice. The times are simulated.
256 devices in a mesh: dp: 32 (over x, z), tensor: 8 (over y, core).
Axes of the slice: x: 4, y: 4, z: 8, core: 2. Of those that a mesh axis runs over, the one named last changes fastest.
Arguments:
- activations: bfloat16 [28672, 1024], P('dp'), may hold values from -6 to 6
- output_grads: bfloat16 [28672, 14784], P('dp', 'tensor'), may hold values from -0.1875 to 0.1875
- error_buffer: bfloat16 [32, 1024, 14784], P('dp', None, 'tensor'), may hold values from -4 to 4
- right_start: bfloat16 [14784, 64], P('tensor'), may hold values from -0.046875 to 0.046875
Outputs:
- left_factor: float32 [1024, 64], replicated
- right_factor: bfloat16 [14784, 64], P('tensor')
- new_error: bfloat16 [32, 1024, 14784], P('dp', None, 'tensor')
All inputs are finite; a program needn't handle non-finite values.
Results may differ from a plain program's by a relative error of at most 0.0062.
Values sent between devices are 32-bit elements; how exact they have to be, the bound alone decides.
No kernel may reach another device: no remote copies, remote signals or barrier semaphores. Data moves between devices by JAX's collectives and lax.ppermute only.
A program may use at most 64 MiB of HBM per device.

v0:
```python
import jax
import jax.numpy as jnp
from jax import lax
from jax.sharding import PartitionSpec as P


def gram_of(matrix):
    return lax.dot_general(
        matrix, matrix, (((0,), (0,)), ((), ())), precision=lax.Precision.HIGHEST
    )


def orthonormal(matrix, lower):
    return jax.scipy.linalg.solve_triangular(lower, matrix.T, lower=True).T


def local(activations, output_grads, error_buffer, right_start):
    gradient = lax.dot_general(
        activations, output_grads, (((0,), (0,)), ((), ())), preferred_element_type=jnp.float32
    )
    accumulated = (error_buffer[0].astype(jnp.float32) + gradient).astype(jnp.bfloat16)
    replicas = lax.axis_size("dp")
    partial_value = jnp.dot(accumulated, right_start, preferred_element_type=jnp.float32)
    summed = lax.psum(partial_value, ("dp", "tensor"))
    left_mean = summed / replicas
    lower = jnp.linalg.cholesky(gram_of(left_mean))
    left_factor = orthonormal(left_mean, lower)
    left_low = left_factor.astype(jnp.bfloat16)
    right_part = lax.dot_general(
        accumulated, left_low, (((0,), (0,)), ((), ())), preferred_element_type=jnp.float32
    )
    right_factor = (lax.psum(right_part, "dp") / replicas).astype(jnp.bfloat16)
    update = lax.dot_general(
        left_low, right_factor, (((1,), (1,)), ((), ())), preferred_element_type=jnp.float32
    )
    new_error = (accumulated.astype(jnp.float32) - update).astype(jnp.bfloat16)
    return (left_factor, right_factor, new_error[None])


def solution(mesh):
    return jax.shard_map(
        local,
        mesh=mesh,
        in_specs=(P("dp", None), P("dp", "tensor"), P("dp", None, "tensor"), P("tensor", None)),
        out_specs=(P(), P("tensor", None), P("dp", None, "tensor")),
        check_vma=False,
    )
```

profile of v0, /device:TPU:32, one launch (start us, length us, event | category | flops | bytes accessed | tf_op | source)
XLA Modules:
  0.0 450.0 jit_solution(5586082167484705631)
XLA Ops:
  7.2 0.0 copy-start
  7.2 0.0 all-reduce.3.cloned.1.call-start
  7.2 1.9 copy-done
  9.1 0.0 copy-start.4
  9.1 6.4 %fusion = bf16[1024,1848]{0,1:T(8,128)(2,1)S(1)} fusion(bf16[896,1024]{1,0:T(8,128)(2,1)} %param.4, bf16[896,1848]{0,1:T(8,128)(2,1)S(1)} %copy-done, bf16[1,1024,1848]{1,2,0:T(8,128)(2,1)} %param.6), kind=kOutput, calls=%fused_computation.1 | convolution fusion | flops 3396771840 | bytes 12716032 | tf_op jit(solution)/shard_map/dot_general | solution.py:18
  15.6 0.0 copy-start.1
  15.6 1.9 copy-done.1
  17.4 0.0 copy-done.4
  17.4 1.5 fusion.16
  19.0 0.0 all-reduce.3.cloned.1.call-update
  19.0 0.0 all-reduce.5.cloned.1.call-start
  19.0 250.7 %all-reduce.3.cloned.1.call-done = f32[1024,64]{0,1:T(8,128)} async-done(((f32[1024,64]{0,1:T(8,128)}), f32[1024,64]{0,1:T(8,128)}) %all-reduce.3.cloned.1.call-update) | async-done | bytes 262160 | tf_op jit(solution)/shard_map/psum | solution.py:24
  269.7 1.4 fusion.4
  271.1 0.1 copy.7
  271.2 5.8 %cholesky.16 = f32[64,64]{1,0:T(8,128)S(1)} custom-call(f32[64,64]{1,0:T(8,128)S(1)} %fusion.13), custom_call_target="Cholesky" | custom-call | tf_op jit(solution)/shard_map/jit(cholesky)/cholesky | solution.py:26
  277.1 0.6 compare_reduce_fusion
  277.7 0.7 fusion.11
  278.4 4.9 %custom-call.7 = f32[1,64,64]{1,2,0:T(8,128)S(1)} custom-call(f32[1,64,64]{2,1,0:T(8,128)S(1)} %fusion.11), custom_call_target="InvertDiagBlocksLowerTriangular" | custom-call | tf_op jit(solution)/shard_map/jit(_solve_triangular)/triangular_solve | solution.py:14
  283.3 1.4 fusion.2
  284.7 0.0 copy-start.2
  284.7 0.7 copy-done.2
  285.4 4.2 fusion.9
  289.6 0.0 all-reduce.5.cloned.1.call-update
  289.6 147.2 %all-reduce.5.cloned.1.call-done = f32[1848,64]{0,1:T(8,128)} async-done(((f32[1848,64]{0,1:T(8,128)}), f32[1848,64]{0,1:T(8,128)}) %all-reduce.5.cloned.1.call-update) | async-done | bytes 473104 | tf_op jit(solution)/shard_map/psum | solution.py:32
  436.8 1.1 multiply_convert_fusion
  437.8 0.0 copy-start.3
  437.8 5.3 %fusion.1 = bf16[1,1024,1848]{1,2,0:T(8,128)(2,1)} fusion(bf16[1848,64]{0,1:T(8,128)(2,1)S(1)} %multiply_convert_fusion, bf16[1024,1848]{0,1:T(8,128)(2,1)} %copy-done.1, f32[1024,64]{0,1:T(8,128)} %copy-done.2), kind=kOutput, calls=%fused_computation.3 | convolution fusion | flops 247963648 | bytes 8068096 | tf_op jit(solution)/shard_map/dot_general | solution.py:33
  443.2 0.0 copy-done.3
  (2 shorter events, 0.0 us)
Async XLA Ops:
  7.2 1.9 copy-start
  7.2 262.5 %all-reduce.3.cloned.1.call-start = ((), (), s32[]{:S(2)}) async-start(), calls=%async_computation | async-start | bytes 524288 | tf_op jit(solution)/shard_map/psum | solution.py:24
  9.1 8.3 %copy-start.4 = (bf16[1848,64]{0,1:T(8,128)(2,1)S(1)}, bf16[1848,64]{0,1:T(8,128)(2,1)}, u32[]{:S(2)}) copy-start(bf16[1848,64]{0,1:T(8,128)(2,1)} %param.7) | copy-start | bytes 709636
  15.6 1.9 copy-start.1
  19.0 417.8 %all-reduce.5.cloned.1.call-start = ((), (), s32[]{:S(2)}) async-start(), calls=%async_computation.1 | async-start | bytes 983040 | tf_op jit(solution)/shard_map/psum | solution.py:32
  284.7 0.7 copy-start.2
  437.8 5.3 %copy-start.3 = (bf16[1848,64]{0,1:T(8,128)(2,1)}, bf16[1848,64]{0,1:T(8,128)(2,1)S(1)}, u32[]{:S(2)}) copy-start(bf16[1848,64]{0,1:T(8,128)(2,1)S(1)} %multiply_convert_fusion) | copy-start | bytes 709636
Sparse Core Ops, SparseCore 0:
  19.1 250.5 all-reduce.2
  289.7 147.0 all-reduce.4
where the time goes:
time: 452 us; the launch traced here: 450 us
  waiting for transfers between devices  398 us (88%)
  matrix products  20.2 us (4%)
  between operations  14.1 us (3%)
  other arithmetic  13.1 us (3%)
  local copies, waits for them, and re-layouts  4.54 us (1%)
    psum x1, waiting for transfers between devices, local(): summed = lax.psum(partial_value, ('dp', 'tensor'))  251 us
    psum x1, waiting for transfers between devices, local(): right_factor = (lax.psum(right_part, 'dp') / replicas).astype(jnp.bfloat16)  147 us
  transfers between devices with their start and end apart: 2, of which 2 were waited for; matrix products, arithmetic and copies ran while one was open for 0% of the time, Pallas kernels for 0%

commit v1 on v0

--- a/solution.py
+++ b/solution.py
@@ -2,6 +2,8 @@
 import jax.numpy as jnp
 from jax import lax
 from jax.sharding import PartitionSpec as P
+
+ALL = ("dp", "tensor")
 
 
 def gram_of(matrix):
@@ -14,22 +16,42 @@
     return jax.scipy.linalg.solve_triangular(lower, matrix.T, lower=True).T
 
 
+def sum_over(pieces, axes):
+    count = pieces.shape[0]
+    arrived = lax.all_to_all(pieces, axes, 0, 0, tiled=True)
+    total = jnp.sum(arrived, axis=0, keepdims=True)
+    return lax.all_to_all(
+        jnp.broadcast_to(total, pieces.shape), axes, 0, 0, tiled=True
+    )
+
+
 def local(activations, output_grads, error_buffer, right_start):
     gradient = lax.dot_general(
         activations, output_grads, (((0,), (0,)), ((), ())), preferred_element_type=jnp.float32
     )
     accumulated = (error_buffer[0].astype(jnp.float32) + gradient).astype(jnp.bfloat16)
     replicas = lax.axis_size("dp")
-    partial_value = jnp.dot(accumulated, right_start, preferred_element_type=jnp.float32)
-    summed = lax.psum(partial_value, ("dp", "tensor"))
+    devices = replicas * lax.axis_size("tensor")
+    rows, rank = accumulated.shape[0], right_start.shape[1]
+    partial_value = lax.dot_general(
+        right_start, accumulated, (((0,), (1,)), ((), ())), preferred_element_type=jnp.float32
+    )
+    blocks = rows // 128
+    pieces = partial_value.reshape(rank, blocks, 128).transpose(1, 0, 2)
+    pieces = pieces.reshape(devices, rank * blocks // devices, 128)
+    summed = sum_over(pieces, ALL).reshape(blocks, rank, 128)
+    summed = summed.transpose(0, 2, 1).reshape(rows, rank)
     left_mean = summed / replicas
     lower = jnp.linalg.cholesky(gram_of(left_mean))
     left_factor = orthonormal(left_mean, lower)
     left_low = left_factor.astype(jnp.bfloat16)
     right_part = lax.dot_general(
-        accumulated, left_low, (((0,), (0,)), ((), ())), preferred_element_type=jnp.float32
+        left_low, accumulated, (((0,), (0,)), ((), ())), preferred_element_type=jnp.float32
     )
-    right_factor = (lax.psum(right_part, "dp") / replicas).astype(jnp.bfloat16)
+    columns = right_part.shape[1]
+    pieces = right_part.reshape(replicas, rank // replicas, columns)
+    right_sum = sum_over(pieces, "dp").reshape(rank, columns)
+    right_factor = (right_sum / replicas).astype(jnp.bfloat16).T
     update = lax.dot_general(
         left_low, right_factor, (((1,), (1,)), ((), ())), preferred_element_type=jnp.float32
     )

time: 452 us -> 138 us (0.31)
  waiting for transfers between devices: 398 us -> 0 us
  blocking collectives: 0 us -> 93.8 us
  between operations: 14.1 us -> 0.75 us
  local copies, waits for them, and re-layouts: 4.54 us -> 9.39 us
    psum x2 -> x0, waiting for transfers between devices: 398 us -> none  [the longest x1 251 us: local(): summed = lax.psum(partial_value, ('dp', 'tensor'))]
    all_to_all x0 -> x4, blocking collectives: none -> 93.8 us  [the longest x2 51.6 us: sum_over(): arrived = lax.all_to_all(pieces, axes, 0, 0, tiled=True)]
  transfers between devices with their start and end apart: 2 -> 0, of which waited for: 2 -> 0; matrix products, arithmetic and copies ran while one was open for 0% -> 0% of each run, Pallas kernels for 0% -> 0%
where the time goes in v1:
time: 138 us
  blocking collectives  93.8 us (68%)
  matrix products  18.5 us (13%)
  other arithmetic  15.5 us (11%)
  local copies, waits for them, and re-layouts  9.39 us (7%)
    all_to_all x2, blocking collectives, sum_over(): arrived = lax.all_to_all(pieces, axes, 0, 0, tiled=True)  51.6 us
    all_to_all x2, blocking collectives, sum_over(): lax.all_to_all(jnp.broadcast_to(total, pieces.shape), axes, 0, 0, tiled=T...  42.1 us
    another operation x3, other arithmetic, local(): lower = jnp.linalg.cholesky(gram_of(left_mean))  6.52 us
    dot_general x1, matrix products, local(): lax.dot_general(activations, output_grads, (((0,), (0,)), ((), ())), pref...  6.45 us
    another operation x2, other arithmetic, orthonormal(): return jax.scipy.linalg.solve_triangular(lower, matrix.T, lower=True).T  5.55 us
    dot_general x1, matrix products, local(): lax.dot_general(left_low, right_factor, (((1,), (1,)), ((), ())), preferr...  5.36 us
    unnamed x10, local copies, waits for them, and re-layouts  5.2 us
    dot_general x1, matrix products, local(): lax.dot_general(left_low, accumulated, (((0,), (0,)), ((), ())), preferre...  4.16 us

profile of v1, /device:TPU:32, one launch (start us, length us, event | category | flops | bytes accessed | tf_op | source)
XLA Modules:
  0.0 137.9 jit_solution(16748143906008492162)
XLA Ops:
  0.6 0.0 copy-start
  0.6 1.9 %copy-done = bf16[896,1848]{0,1:T(8,128)(2,1)S(1)} copy-done((bf16[896,1848]{0,1:T(8,128)(2,1)S(1)}, bf16[896,1848]{0,1:T(8,128)(2,1)}, u32[]{:S(2)}) %copy-start) | copy-done | bytes 3311640
  2.6 0.0 copy-start.4
  2.6 6.5 %fusion = bf16[1024,1848]{0,1:T(8,128)(2,1)S(1)} fusion(bf16[896,1024]{1,0:T(8,128)(2,1)} %param.4, bf16[896,1848]{0,1:T(8,128)(2,1)S(1)} %copy-done, bf16[1,1024,1848]{1,2,0:T(8,128)(2,1)} %param.6), kind=kOutput, calls=%fused_computation.1 | convolution fusion | flops 3396771840 | bytes 12716032 | tf_op jit(solution)/shard_map/dot_general | solution.py:29
  9.0 0.0 copy-start.1
  9.0 1.9 %copy-done.1 = bf16[1024,1848]{0,1:T(8,128)(2,1)} copy-done((bf16[1024,1848]{0,1:T(8,128)(2,1)}, bf16[1024,1848]{0,1:T(8,128)(2,1)S(1)}, u32[]{:S(2)}) %copy-start.1) | copy-done | bytes 3784728
  10.9 0.0 copy-done.4
  10.9 0.8 convolution_bitcast_fusion
  11.8 28.7 %all_to_all.20 = f32[256,2,128]{2,1,0:T(2,128)} all-to-all(f32[256,2,128]{2,1,0:T(2,128)S(1)} %bitcast.43), channel_id=1, replica_groups=mesh['dp'=32,'tensor'=8] {'dp','tensor'}, dimensions={0} | all-to-all | bytes 524288 | tf_op jit(solution)/shard_map/all_to_all | solution.py:21
  40.4 1.2 reduce_sum.18
  41.6 0.1 broadcast_in_dim.8
  41.7 20.6 %all_to_all.21 = f32[256,2,128]{2,1,0:T(2,128)S(1)} all-to-all(f32[256,2,128]{2,1,0:T(2,128)S(1)} %broadcast_in_dim.8), channel_id=1, replica_groups=mesh['dp'=32,'tensor'=8] {'dp','tensor'}, dimensions={0} | all-to-all | bytes 524288 | tf_op jit(solution)/shard_map/all_to_all | solution.py:23
  62.3 0.1 broadcast_multiply_fusion
  62.5 0.0 copy-start.2
  62.5 0.7 copy-done.2
  63.2 0.4 convolution_bitcast_fusion.1
  63.5 0.1 copy.10
  63.6 5.8 %cholesky.16 = f32[64,64]{1,0:T(8,128)S(1)} custom-call(f32[64,64]{1,0:T(8,128)S(1)} %fusion.10), custom_call_target="Cholesky" | custom-call | tf_op jit(solution)/shard_map/jit(cholesky)/cholesky | solution.py:45
  69.5 0.6 compare_reduce_fusion
  70.1 0.7 fusion.8
  70.8 4.9 %custom-call.7 = f32[1,64,64]{1,2,0:T(8,128)S(1)} custom-call(f32[1,64,64]{2,1,0:T(8,128)S(1)} %fusion.8), custom_call_target="InvertDiagBlocksLowerTriangular" | custom-call | tf_op jit(solution)/shard_map/jit(_solve_triangular)/triangular_solve | solution.py:16
  75.7 1.4 %fusion.2 = f32[1024,64]{0,1:T(8,128)S(1)} fusion(f32[8,8,8,128]{3,2,1,0:T(8,128)} %bitcast.42, f32[1,64,64]{1,2,0:T(8,128)S(1)} %custom-call.7), kind=kOutput, calls=%fused_computation.7 | convolution fusion | flops 50331648 | bytes 540672 | tf_op jit(solution)/shard_map/jit(_solve_triangular)/triangular_solve | solution.py:16
  77.1 0.0 copy-start.3
  77.1 0.7 copy-done.3
  77.8 4.2 %fusion.6 = f32[64,1848]{1,0:T(8,128)} fusion(bf16[1024,1848]{0,1:T(8,128)(2,1)} %copy-done.1, f32[1024,64]{0,1:T(8,128)S(1)} %fusion.2), kind=kOutput, calls=%fused_computation.13 | convolution fusion | flops 242286592 | bytes 4519936 | tf_op jit(solution)/shard_map/dot_general | solution.py:48
  82.0 2.1 %reshape.42 = f32[32,2,1848]{2,1,0:T(2,128)} reshape(f32[64,1848]{1,0:T(8,128)} %fusion.6) | data formatting | bytes 946176 | tf_op jit(solution)/shard_map/reshape | solution.py:52
  84.0 23.0 %all_to_all.22 = f32[32,2,1848]{2,1,0:T(2,128)} all-to-all(f32[32,2,1848]{2,1,0:T(2,128)} %reshape.42), channel_id=1, replica_groups=mesh['dp'=32,'tensor'=8] {'dp'}, dimensions={0} | all-to-all | bytes 946176 | tf_op jit(solution)/shard_map/all_to_all | solution.py:21
  107.0 1.2 reduce_sum.19
  108.2 0.1 broadcast_in_dim.9
  108.3 21.5 %all_to_all.23 = f32[32,2,1848]{2,1,0:T(2,128)S(1)} all-to-all(f32[32,2,1848]{2,1,0:T(2,128)S(1)} %broadcast_in_dim.9), channel_id=1, replica_groups=mesh['dp'=32,'tensor'=8] {'dp'}, dimensions={0} | all-to-all | bytes 946176 | tf_op jit(solution)/shard_map/all_to_all | solution.py:23
  129.9 0.9 multiply_convert_fusion
  130.7 1.8 %convert_element_type.29 = bf16[64,1848]{1,0:T(8,128)(2,1)} reshape(bf16[32,2,1848]{2,1,0:T(2,128)(2,1)} %multiply_convert_fusion) | data formatting | bytes 473088 | tf_op jit(solution)/shard_map/convert_element_type | solution.py:54
  132.6 5.4 %fusion.1 = bf16[1,1024,1848]{1,2,0:T(8,128)(2,1)} fusion(bf16[64,1848]{1,0:T(8,128)(2,1)} %convert_element_type.29, bf16[1024,1848]{0,1:T(8,128)(2,1)} %copy-done.1, f32[1024,64]{0,1:T(8,128)} %copy-done.3), kind=kOutput, calls=%fused_computation.3 | convolution fusion | flops 247963648 | bytes 8068096 | tf_op jit(solution)/shard_map/dot_general | solution.py:55
  (3 shorter events, 0.1 us)
Async XLA Ops:
  0.6 1.9 %copy-start = (bf16[896,1848]{0,1:T(8,128)(2,1)S(1)}, bf16[896,1848]{0,1:T(8,128)(2,1)}, u32[]{:S(2)}) copy-start(bf16[896,1848]{0,1:T(8,128)(2,1)} %param.5) | copy-start | bytes 9934852
  2.6 8.3 %copy-start.4 = (bf16[1848,64]{0,1:T(8,128)(2,1)S(1)}, bf16[1848,64]{0,1:T(8,128)(2,1)}, u32[]{:S(2)}) copy-start(bf16[1848,64]{0,1:T(8,128)(2,1)} %param.7) | copy-start | bytes 709636
  9.0 1.9 %copy-start.1 = (bf16[1024,1848]{0,1:T(8,128)(2,1)}, bf16[1024,1848]{0,1:T(8,128)(2,1)S(1)}, u32[]{:S(2)}) copy-start(bf16[1024,1848]{0,1:T(8,128)(2,1)S(1)} %fusion) | copy-start | bytes 11354116
  62.5 0.7 copy-start.2
  77.1 0.7 copy-start.3

commit v2 on v0

v2 whole, which is shorter than its diff:
```python
import functools

import jax
import jax.numpy as jnp
from jax import lax
from jax.experimental import pallas as pl
from jax.experimental.pallas import tpu as pltpu
from jax.sharding import Mesh, PartitionSpec as P

ROWS, COLS, RANK, TOK, N_DP = 1024, 1848, 64, 896, 32
LANES = 128
ROW_TILES = ROWS // LANES
COL_TILES = -(-COLS // LANES)
HALF = 1024
HALVES = (HALF, COLS - HALF)
CHUNKS = ((0, 0, 512), (0, 512, 512), (1, 0, 512), (1, 512, COLS - HALF - 512))
DP = ("x", "z")
PLANE = ("x", "y", "core")
VMEM_LIMIT = 53 * 2**20
LEFT_LIMIT = 56 * 2**20
HIGHEST = lax.Precision.HIGHEST
ANY = pl.BlockSpec(memory_space=pl.ANY)
WHOLE = pl.BlockSpec(memory_space=pltpu.VMEM)


def params(limit=VMEM_LIMIT):
    return pltpu.CompilerParams(vmem_limit_bytes=limit)


def split(value):
    high = value.astype(jnp.bfloat16)
    rest = value - high.astype(jnp.float32)
    middle = rest.astype(jnp.bfloat16)
    low = (rest - middle.astype(jnp.float32)).astype(jnp.bfloat16)
    return high, middle, low


def add_parts(product):
    return product[:RANK] + (product[RANK : 2 * RANK] + product[2 * RANK :])


def whole_copies(sources, targets, sems):
    return [
        pltpu.make_async_copy(source, target, sems.at[i])
        for i, (source, target) in enumerate(zip(sources, targets))
    ]


def left_kernel(
    act_hbm, grad_hbm, error_hbm, right_hbm, left_ref,
    act_ref, grad_ref, error_ref, right_ref, sems,
):
    act_copy, grad_copy, error_copy, right_copy = whole_copies(
        (act_hbm, grad_hbm, error_hbm, right_hbm),
        (act_ref, grad_ref, error_ref, right_ref),
        sems,
    )
    right_copy.start()
    grad_copy.start()
    act_copy.start()
    error_copy.start()
    right_copy.wait()
    grad_copy.wait()
    inner = jnp.dot(right_ref[...], grad_ref[...], preferred_element_type=jnp.float32)
    parts = jnp.concatenate(split(inner), axis=0)
    act_copy.wait()
    total = add_parts(jnp.dot(parts, act_ref[...], preferred_element_type=jnp.float32))
    error_copy.wait()
    total = total + jnp.dot(right_ref[...], error_ref[...], preferred_element_type=jnp.float32)
    for tile in range(ROW_TILES):
        left_ref[pl.ds(tile * RANK, RANK), :] = total[:, tile * LANES : (tile + 1) * LANES]


def left_term(act, grad, error, right):
    return pl.pallas_call(
        left_kernel,
        in_specs=[ANY] * 4,
        out_specs=WHOLE,
        out_shape=jax.ShapeDtypeStruct((ROW_TILES * RANK, LANES), jnp.float32),
        scratch_shapes=[
            pltpu.VMEM((TOK, ROWS), jnp.bfloat16),
            pltpu.VMEM((COLS, TOK), jnp.bfloat16),
            pltpu.VMEM((COLS, ROWS), jnp.bfloat16),
            pltpu.VMEM((RANK, COLS), jnp.bfloat16),
            pltpu.SemaphoreType.DMA((4,)),
        ],
        compiler_params=params(LEFT_LIMIT),
        cost_estimate=pl.CostEstimate(
            flops=2 * RANK * (COLS * (ROWS + TOK) + ROWS * TOK),
            bytes_accessed=9_000_000, transcendentals=0,
        ),
        name="left_term",
    )(act, grad, error, right)


def accumulate_kernel(
    half, act_hbm, grad_hbm, error_hbm, acc_hbm,
    act_ref, grad_ref, error_ref, acc_ref, sems, grad_sems, error_sems, acc_sems,
):
    chunks = [(i, a, n) for i, (h, a, n) in enumerate(c for c in CHUNKS if c[0] == half)]
    act_copy = pltpu.make_async_copy(act_hbm, act_ref, sems.at[0])
    grad_copies, error_copies, acc_copies = [], [], []
    act_copy.start()
    for i, a, n in chunks:
        here, there = pl.ds(a, n), pl.ds(half * HALF + a, n)
        grad_copies.append(
            pltpu.make_async_copy(grad_hbm.at[there], grad_ref.at[here], grad_sems.at[i])
        )
        error_copies.append(
            pltpu.make_async_copy(error_hbm.at[there], error_ref.at[here], error_sems.at[i])
        )
        acc_copies.append(
            pltpu.make_async_copy(acc_ref.at[here], acc_hbm.at[here], acc_sems.at[i])
        )
        grad_copies[i].start()
        error_copies[i].start()
    act_copy.wait()
    for i, a, n in chunks:
        rows = pl.ds(a, n)
        grad_copies[i].wait()
        gradient = jnp.dot(grad_ref[rows, :], act_ref[...], preferred_element_type=jnp.float32)
        error_copies[i].wait()
        acc_ref[rows, :] = (error_ref[rows, :].astype(jnp.float32) + gradient).astype(jnp.bfloat16)
        acc_copies[i].start()
    for copy in acc_copies:
        copy.wait()


def accumulate(half, act, grad, error):
    size = HALVES[half]
    return pl.pallas_call(
        functools.partial(accumulate_kernel, half),
        in_specs=[ANY] * 3,
        out_specs=ANY,
        out_shape=jax.ShapeDtypeStruct((size, ROWS), jnp.bfloat16),
        scratch_shapes=[
            pltpu.VMEM((TOK, ROWS), jnp.bfloat16),
            pltpu.VMEM((size, TOK), jnp.bfloat16),
            pltpu.VMEM((size, ROWS), jnp.bfloat16),
            pltpu.VMEM((size, ROWS), jnp.bfloat16),
            pltpu.SemaphoreType.DMA((1,)),
            pltpu.SemaphoreType.DMA((2,)),
            pltpu.SemaphoreType.DMA((2,)),
            pltpu.SemaphoreType.DMA((2,)),
        ],
        compiler_params=params(56 * 2**20),
        cost_estimate=pl.CostEstimate(
            flops=2 * size * ROWS * TOK, bytes_accessed=8_000_000, transcendentals=0
        ),
        name="accumulate",
    )(act, grad, error)


def chunk_copies(sources, targets, sems):
    return [
        pltpu.make_async_copy(
            sources[h].at[pl.ds(a, n)], targets[h].at[pl.ds(a, n)], sems.at[i]
        )
        for i, (h, a, n) in enumerate(CHUNKS)
    ]


def project_kernel(left_ref, acc_a, acc_b, out_ref, parts_ref, half_a, half_b, sems):
    acc = (half_a, half_b)
    copies = chunk_copies((acc_a, acc_b), acc, sems)
    for copy in copies:
        copy.start()
    for tile in range(ROW_TILES):
        lanes = pl.ds(tile * LANES, LANES)
        mean = left_ref[pl.ds(tile * RANK, RANK), :] * (1.0 / N_DP)
        for i, part in enumerate(split(mean)):
            parts_ref[pl.ds(i * RANK, RANK), lanes] = part
    parts = parts_ref[...]
    for i, (h, a, n) in enumerate(CHUNKS):
        copies[i].wait()
        product = lax.dot_general(
            parts, acc[h][pl.ds(a, n), :], (((1,), (1,)), ((), ())),
            preferred_element_type=jnp.float32,
        )
        total = add_parts(product)
        for tile in range(-(-n // LANES)):
            piece = total[:, tile * LANES : min(n, (tile + 1) * LANES)]
            spare = LANES - piece.shape[1]
            if spare:
                piece = jnp.concatenate([piece, jnp.zeros((RANK, spare), jnp.float32)], axis=1)
            out_ref[pl.ds(((h * HALF + a) // LANES + tile) * RANK, RANK), :] = piece


def project(left_sum, acc_a, acc_b):
    return pl.pallas_call(
        project_kernel,
        in_specs=[WHOLE, ANY, ANY],
        out_specs=WHOLE,
        out_shape=jax.ShapeDtypeStruct((COL_TILES * RANK, LANES), jnp.float32),
        scratch_shapes=[
            pltpu.VMEM((3 * RANK, ROWS), jnp.bfloat16),
            pltpu.VMEM((HALVES[0], ROWS), jnp.bfloat16),
            pltpu.VMEM((HALVES[1], ROWS), jnp.bfloat16),
            pltpu.SemaphoreType.DMA((len(CHUNKS),)),
        ],
        compiler_params=params(),
        cost_estimate=pl.CostEstimate(
            flops=6 * COLS * ROWS * RANK, bytes_accessed=4_500_000, transcendentals=0
        ),
        name="project",
    )(left_sum, acc_a, acc_b)


def finish_kernel(
    sum_ref, inverse_ref, left_ref, acc_a, acc_b, right_hbm, error_hbm,
    half_a, half_b, right_ref, error_ref, sems, right_sem, error_sems,
):
    acc = (half_a, half_b)
    copies = chunk_copies((acc_a, acc_b), acc, sems)
    starts = [h * HALF + a for h, a, n in CHUNKS]
    error_copies = [
        pltpu.make_async_copy(
            error_ref.at[pl.ds(start, chunk[2])],
            error_hbm.at[pl.ds(start, chunk[2])],
            error_sems.at[i],
        )
        for i, (start, chunk) in enumerate(zip(starts, CHUNKS))
    ]
    right_copy = pltpu.make_async_copy(right_ref, right_hbm, right_sem.at[0])
    for copy in copies:
        copy.start()
    terms = jnp.concatenate(
        [sum_ref[pl.ds(tile * RANK, RANK), :] for tile in range(COL_TILES)], axis=1
    )
    right = jnp.dot(
        inverse_ref[...], terms, precision=HIGHEST, preferred_element_type=jnp.float32
    )
    right = (right * (1.0 / N_DP)).astype(jnp.bfloat16)
    right_ref[...] = right[:, :COLS]
    right_copy.start()
    left = left_ref[...]
    for i, (h, a, n) in enumerate(CHUNKS):
        start = starts[i]
        update = lax.dot_general(
            right_ref[:, start : start + n], left, (((0,), (0,)), ((), ())),
            preferred_element_type=jnp.float32,
        )
        copies[i].wait()
        held = acc[h][pl.ds(a, n), :].astype(jnp.float32)
        error_ref[pl.ds(start, n), :] = (held - update).astype(jnp.bfloat16)
        error_copies[i].start()
    right_copy.wait()
    for copy in error_copies:
        copy.wait()


def finish(right_sum, inverse, left_low, acc_a, acc_b):
    return pl.pallas_call(
        finish_kernel,
        in_specs=[WHOLE, WHOLE, WHOLE, ANY, ANY],
        out_specs=[ANY, ANY],
        out_shape=[
            jax.ShapeDtypeStruct((RANK, COLS), jnp.bfloat16),
            jax.ShapeDtypeStruct((COLS, ROWS), jnp.bfloat16),
        ],
        scratch_shapes=[
            pltpu.VMEM((HALVES[0], ROWS), jnp.bfloat16),
            pltpu.VMEM((HALVES[1], ROWS), jnp.bfloat16),
            pltpu.VMEM((RANK, COLS), jnp.bfloat16),
            pltpu.VMEM((COLS, ROWS), jnp.bfloat16),
            pltpu.SemaphoreType.DMA((len(CHUNKS),)),
            pltpu.SemaphoreType.DMA((1,)),
            pltpu.SemaphoreType.DMA((len(CHUNKS),)),
        ],
        compiler_params=params(),
        cost_estimate=pl.CostEstimate(
            flops=2 * COLS * ROWS * RANK, bytes_accessed=8_500_000, transcendentals=0
        ),
        name="finish",
    )(right_sum, inverse, left_low, acc_a, acc_b)


def exchange(pieces, axes):
    return lax.all_to_all(pieces, axes, 0, 0, tiled=True)


def spread(total, count):
    return jnp.broadcast_to(total[None], (count,) + total.shape)


def sum_left(part, work):
    mine = jnp.sum(exchange(part.reshape(32, 16, LANES), PLANE), axis=0)
    mine, first = lax.optimization_barrier((mine, work[0]))
    mine = jnp.sum(exchange(spread(mine, 8), "z"), axis=0)
    mine, second = lax.optimization_barrier((mine, work[1]))
    return exchange(spread(mine, 32), PLANE).reshape(part.shape), (first, second)


def sum_right(part):
    mine = jnp.sum(exchange(part.reshape(32, 15, 2, LANES), DP), axis=0)
    return exchange(spread(mine, 32), DP).reshape(part.shape)


def orthonormal(left_sum):
    mean = left_sum.reshape(ROW_TILES, RANK, LANES).transpose(1, 0, 2).reshape(RANK, ROWS)
    mean = mean / N_DP
    gram = lax.dot_general(mean, mean, (((1,), (1,)), ((), ())), precision=HIGHEST)
    lower = jnp.linalg.cholesky(gram)
    inverse = jax.scipy.linalg.solve_triangular(lower, jnp.eye(RANK, dtype=jnp.float32), lower=True)
    return inverse, jnp.dot(inverse, mean, precision=HIGHEST)


def local(activations, output_grads, error_buffer, right_start):
    grad, error = output_grads.T, error_buffer[0].T
    left_part = left_term(activations, grad, error, right_start.T)
    acc = [accumulate(half, activations, grad, error) for half in range(2)]
    left_sum, acc = sum_left(left_part, acc)
    right_sum = sum_right(project(left_sum, *acc))
    inverse, left = orthonormal(left_sum)
    right, new_error = finish(right_sum, inverse, left.astype(jnp.bfloat16), *acc)
    return (left.T, right.T, new_error.T[None])


def solution(mesh):
    fine = Mesh(mesh.devices.reshape(4, 8, 4, 2), ("x", "z", "y", "core"))
    tensor = ("y", "core")
    return jax.shard_map(
        local,
        mesh=fine,
        in_specs=(P(DP, None), P(DP, tensor), P(DP, None, tensor), P(tensor, None)),
        out_specs=(P(), P(tensor, None), P(DP, None, tensor)),
        check_vma=False,
    )
```

time: 452 us -> 108 us (0.24)
  waiting for transfers between devices: 398 us -> 24.8 us
  starting transfers between devices: 0.08 us -> 27.3 us
  Pallas kernels: 0 us -> 25.9 us
  matrix products: 20.2 us -> 1.65 us
  blocking collectives: 0 us -> 13.3 us
  between operations: 14.1 us -> 0.91 us
    psum x2 -> x0, waiting for transfers between devices: 398 us -> none  [the longest x1 251 us: local(): summed = lax.psum(partial_value, ('dp', 'tensor'))]
    all_to_all x0 -> x4, starting transfers between devices: none -> 27.3 us  [exchange(): return lax.all_to_all(pieces, axes, 0, 0, tiled=True)]
    pallas_call x0 -> x5, Pallas kernels: none -> 25.9 us  [the longest x2 11.4 us: accumulate(): pl.pallas_call(functools.partial(accumulate_kernel, half), in_specs=[ANY]...]
    all_to_all x0 -> x4, waiting for transfers between devices: none -> 24.8 us  [exchange(): return lax.all_to_all(pieces, axes, 0, 0, tiled=True)]
    dot_general x5 -> x2, matrix products: 18.8 us -> 1.42 us  [the longest x1 1.06 us: orthonormal(): return (inverse, jnp.dot(inverse, mean, precision=HIGHEST))]
    all_to_all x0 -> x1, blocking collectives: none -> 13.3 us  [exchange(): return lax.all_to_all(pieces, axes, 0, 0, tiled=True)]
  transfers between devices with their start and end apart: 2 -> 4, of which waited for: 2 -> 4; matrix products, arithmetic and copies ran while one was open for 0% -> 13% of each run, Pallas kernels for 0% -> 11%
where the time goes in v2:
time: 108 us
  starting transfers between devices  27.3 us (25%)
  Pallas kernels  25.9 us (24%)
  waiting for transfers between devices  24.8 us (23%)
  blocking collectives  13.3 us (12%)
  other arithmetic  12.3 us (11%)
  matrix products  1.65 us (2%)
  local copies, waits for them, and re-layouts  1.63 us (2%)
    all_to_all x4, starting transfers between devices, exchange(): return lax.all_to_all(pieces, axes, 0, 0, tiled=True)  27.3 us
    all_to_all x4, waiting for transfers between devices, exchange(): return lax.all_to_all(pieces, axes, 0, 0, tiled=True)  24.8 us
    all_to_all x1, blocking collectives, exchange(): return lax.all_to_all(pieces, axes, 0, 0, tiled=True)  13.3 us
    pallas_call x2, Pallas kernels, accumulate(): pl.pallas_call(functools.partial(accumulate_kernel, half), in_specs=[ANY]...  11.4 us
    another operation x3, other arithmetic, orthonormal(): lower = jnp.linalg.cholesky(gram)  6.52 us
    another operation x2, other arithmetic, orthonormal(): jax.scipy.linalg.solve_triangular(lower, jnp.eye(RANK, dtype=jnp.float32)...  5.55 us
    pallas_call x1, Pallas kernels, left_term(): pl.pallas_call(left_kernel, in_specs=[ANY] * 4, out_specs=WHOLE, out_shap...  5.29 us
    pallas_call x1, Pallas kernels, finish(): pl.pallas_call(finish_kernel, in_specs=[WHOLE, WHOLE, WHOLE, ANY, ANY], o...  5.17 us
  transfers between devices with their start and end apart: 4, of which 4 were waited for; matrix products, arithmetic and copies ran while one was open for 13% of the time, Pallas kernels for 11%

profile of v2, /device:TPU:32, one launch (start us, length us, event | category | flops | bytes accessed | tf_op | source)
XLA Modules:
  0.0 107.8 jit_solution(14778028425927539429)
XLA Ops:
  0.6 5.3 %left_term.1 = f32[512,128]{1,0:T(8,128)} custom-call(bf16[896,1024]{1,0:T(8,128)(2,1)} %act_hbm.5, bf16[1848,896]{1,0:T(8,128)(2,1)} %bitcast.42, bf16[1848,1024]{1,0:T(8,128)(2,1)} %bitcast.39, bf16[64,1848]{1,0:T(8,128)(2,1)} %bitcast.49), custom_call_target="tpu_custom_call" | custom-call | flops 571604992 | bytes 9000000 | tf_op jit(solution)/shard_map/left_term/pallas_call | solution.py:75
  5.9 7.3 %all-to-all-start = ((f32[32,16,128]{2,1,0:T(8,128)}), f32[32,16,128]{2,1,0:T(8,128)S(1)}, u32[]{:S(2)}, u32[]{:S(2)}) async-start(f32[32,16,128]{2,1,0:T(8,128)} %bitcast.47), calls=%async_computation | async-start | bytes 524288 | tf_op jit(solution)/shard_map/all_to_all | solution.py:279
  13.3 6.0 %accumulate.2.acc_a = bf16[1024,1024]{1,0:T(8,128)(2,1)} custom-call(bf16[896,1024]{1,0:T(8,128)(2,1)} %act_hbm.5, bf16[1848,896]{1,0:T(8,128)(2,1)} %bitcast.43, bf16[1848,1024]{1,0:T(8,128)(2,1)} %bitcast.40), custom_call_target="tpu_custom_call" | custom-call | flops 1879048192 | bytes 8000000 | tf_op jit(solution)/shard_map/accumulate/pallas_call | solution.py:131
  19.3 2.9 %all-to-all-done = f32[32,16,128]{2,1,0:T(8,128)S(1)} async-done(((f32[32,16,128]{2,1,0:T(8,128)}), f32[32,16,128]{2,1,0:T(8,128)S(1)}, u32[]{:S(2)}, u32[]{:S(2)}) %all-to-all-start) | async-done | bytes 262176 | tf_op jit(solution)/shard_map/all_to_all | solution.py:279
  22.2 0.6 broadcast_in_dim.9
  22.9 8.6 %all-to-all-start.1 = ((f32[8,16,128]{2,1,0:T(8,128)}), f32[8,16,128]{2,1,0:T(8,128)S(1)}, u32[]{:S(2)}, u32[]{:S(2)}) async-start(f32[8,16,128]{2,1,0:T(8,128)} %broadcast_in_dim.9), calls=%async_computation.1 | async-start | bytes 131072 | tf_op jit(solution)/shard_map/all_to_all | solution.py:279
  31.4 5.4 %accumulate.3.acc_b = bf16[824,1024]{1,0:T(8,128)(2,1)} custom-call(bf16[896,1024]{1,0:T(8,128)(2,1)} %act_hbm.5, bf16[1848,896]{1,0:T(8,128)(2,1)} %bitcast.44, bf16[1848,1024]{1,0:T(8,128)(2,1)} %bitcast.41), custom_call_target="tpu_custom_call" | custom-call | flops 1512046592 | bytes 8000000 | tf_op jit(solution)/shard_map/accumulate/pallas_call | solution.py:131
  36.8 1.5 %all-to-all-done.1 = f32[8,16,128]{2,1,0:T(8,128)S(1)} async-done(((f32[8,16,128]{2,1,0:T(8,128)}), f32[8,16,128]{2,1,0:T(8,128)S(1)}, u32[]{:S(2)}, u32[]{:S(2)}) %all-to-all-start.1) | async-done | bytes 65568 | tf_op jit(solution)/shard_map/all_to_all | solution.py:279
  38.4 13.3 %all_to_all.25 = f32[32,16,128]{2,1,0:T(8,128)S(1)} all-to-all(f32[32,16,128]{2,1,0:T(8,128)S(1)} %broadcast_in_dim.10), channel_id=1, replica_groups=mesh['x'=4,'z'=8,'y'=4,'core'=2] {'x','y','core'}, dimensions={0} | all-to-all | bytes 524288 | tf_op jit(solution)/shard_map/all_to_all | solution.py:279
  51.7 4.0 %project.1 = f32[960,128]{1,0:T(8,128)} custom-call(f32[512,128]{1,0:T(8,128)S(1)} %bitcast.37, bf16[1024,1024]{1,0:T(8,128)(2,1)} %accumulate.2.acc_a, bf16[824,1024]{1,0:T(8,128)(2,1)} %accumulate.3.acc_b), custom_call_target="tpu_custom_call" | custom-call | flops 726663168 | bytes 4500000 | tf_op jit(solution)/shard_map/project/pallas_call | solution.py:190
  55.7 6.6 %all-to-all-start.3 = ((f32[32,15,2,128]{3,2,1,0:T(2,128)}), f32[32,15,2,128]{3,2,1,0:T(2,128)S(1)}, u32[]{:S(2)}, u32[]{:S(2)}) async-start(f32[32,15,2,128]{3,2,1,0:T(2,128)} %bitcast.15), calls=%async_computation.3 | async-start | bytes 983040 | tf_op jit(solution)/shard_map/all_to_all | solution.py:279
  62.3 0.4 convolution_bitcast_fusion
  62.7 0.1 copy.10
  62.8 16.9 %all-to-all-done.3 = f32[32,15,2,128]{3,2,1,0:T(2,128)S(1)} async-done(((f32[32,15,2,128]{3,2,1,0:T(2,128)}), f32[32,15,2,128]{3,2,1,0:T(2,128)S(1)}, u32[]{:S(2)}, u32[]{:S(2)}) %all-to-all-start.3) | async-done | bytes 491552 | tf_op jit(solution)/shard_map/all_to_all | solution.py:279
  79.7 0.2 reduce_sum.29
  79.9 0.9 broadcast_in_dim.11
  80.8 4.8 %all-to-all-start.4 = ((f32[32,15,2,128]{3,2,1,0:T(2,128)}), f32[32,15,2,128]{3,2,1,0:T(2,128)S(1)}, u32[]{:S(2)}, u32[]{:S(2)}) async-start(f32[32,15,2,128]{3,2,1,0:T(2,128)} %broadcast_in_dim.11), calls=%async_computation.4 | async-start | bytes 983040 | tf_op jit(solution)/shard_map/all_to_all | solution.py:279
  85.6 5.8 %cholesky.17 = f32[64,64]{1,0:T(8,128)S(1)} custom-call(f32[64,64]{1,0:T(8,128)S(1)} %fusion.6), custom_call_target="Cholesky" | custom-call | tf_op jit(solution)/shard_map/jit(cholesky)/cholesky | solution.py:303
  91.5 0.6 compare_reduce_fusion
  92.1 0.7 fusion.3
  92.8 4.9 %custom-call.7 = f32[1,64,64]{1,2,0:T(8,128)S(1)} custom-call(f32[1,64,64]{2,1,0:T(8,128)S(1)} %fusion.3), custom_call_target="InvertDiagBlocksLowerTriangular" | custom-call | tf_op jit(solution)/shard_map/jit(_solve_triangular)/triangular_solve | solution.py:304
  97.7 0.2 fusion.4.inverse_ref
  97.9 1.1 fusion.7
  99.0 3.4 %all-to-all-done.4 = f32[32,15,2,128]{3,2,1,0:T(2,128)S(1)} async-done(((f32[32,15,2,128]{3,2,1,0:T(2,128)}), f32[32,15,2,128]{3,2,1,0:T(2,128)S(1)}, u32[]{:S(2)}, u32[]{:S(2)}) %all-to-all-start.4) | async-done | bytes 491552 | tf_op jit(solution)/shard_map/all_to_all | solution.py:279
  102.4 5.2 %finish.1 = (bf16[64,1848]{1,0:T(8,128)(2,1)}, bf16[1848,1024]{1,0:T(8,128)(2,1)}) custom-call(f32[960,128]{1,0:T(8,128)S(1)} %bitcast.38, f32[64,64]{1,0:T(8,128)S(1)} %fusion.4.inverse_ref, bf16[64,1024]{1,0:T(8,128)(2,1)S(1)} %get-tuple-element.15.left_ref, bf16[1024,1024]{1,0:T(8,128)(2,1)} %accumulate.2.acc_a, bf16[824,1024]{1,0:T(8,128)(2,1)} %accumulate.3.acc_b), custom_call_target="tpu_custom_call" | custom-call | flops 242221056 | bytes 8500000 | tf_op jit(solution)/shard_map/finish/pallas_call | solution.py:253
  (6 shorter events, 0.1 us)
Async XLA Ops:
  5.9 16.3 %all-to-all-start = ((f32[32,16,128]{2,1,0:T(8,128)}), f32[32,16,128]{2,1,0:T(8,128)S(1)}, u32[]{:S(2)}, u32[]{:S(2)}) async-start(f32[32,16,128]{2,1,0:T(8,128)} %bitcast.47), calls=%async_computation | async-start | bytes 524288 | tf_op jit(solution)/shard_map/all_to_all | solution.py:279
  22.9 15.5 %all-to-all-start.1 = ((f32[8,16,128]{2,1,0:T(8,128)}), f32[8,16,128]{2,1,0:T(8,128)S(1)}, u32[]{:S(2)}, u32[]{:S(2)}) async-start(f32[8,16,128]{2,1,0:T(8,128)} %broadcast_in_dim.9), calls=%async_computation.1 | async-start | bytes 131072 | tf_op jit(solution)/shard_map/all_to_all | solution.py:279
  55.7 24.1 %all-to-all-start.3 = ((f32[32,15,2,128]{3,2,1,0:T(2,128)}), f32[32,15,2,128]{3,2,1,0:T(2,128)S(1)}, u32[]{:S(2)}, u32[]{:S(2)}) async-start(f32[32,15,2,128]{3,2,1,0:T(2,128)} %bitcast.15), calls=%async_computation.3 | async-start | bytes 983040 | tf_op jit(solution)/shard_map/all_to_all | solution.py:279
  80.8 21.6 %all-to-all-start.4 = ((f32[32,15,2,128]{3,2,1,0:T(2,128)}), f32[32,15,2,128]{3,2,1,0:T(2,128)S(1)}, u32[]{:S(2)}, u32[]{:S(2)}) async-start(f32[32,15,2,128]{3,2,1,0:T(2,128)} %broadcast_in_dim.11), calls=%async_computation.4 | async-start | bytes 983040 | tf_op jit(solution)/shard_map/all_to_all | solution.py:279

commit v3 on v2

v3 whole, which is shorter than its diff:
```python
import functools

import jax
import jax.numpy as jnp
from jax import lax
from jax.experimental import pallas as pl
from jax.experimental.pallas import tpu as pltpu
from jax.sharding import Mesh, PartitionSpec as P

ROWS, COLS, RANK, TOK, N_DP = 1024, 1848, 64, 896, 32
LANES = 128
ROW_TILES = ROWS // LANES
COL_TILES = -(-COLS // LANES)
HALF = 1024
HALVES = (HALF, COLS - HALF)
CHUNKS = ((0, 0, 512), (0, 512, 512), (1, 0, 512), (1, 512, COLS - HALF - 512))
Z = ("zh", "zl")
DP = ("x",) + Z
NEAR = ("x", "zl")
PLANE = ("x", "y", "core")
VMEM_LIMIT = 53 * 2**20
LEFT_LIMIT = 56 * 2**20
ACC_LIMIT = 49 * 2**20
HIGHEST = lax.Precision.HIGHEST
PIVOTS = 8
ANY = pl.BlockSpec(memory_space=pl.ANY)
WHOLE = pl.BlockSpec(memory_space=pltpu.VMEM)


def params(limit=VMEM_LIMIT):
    return pltpu.CompilerParams(vmem_limit_bytes=limit)


def split(value):
    high = value.astype(jnp.bfloat16)
    rest = value - high.astype(jnp.float32)
    middle = rest.astype(jnp.bfloat16)
    low = (rest - middle.astype(jnp.float32)).astype(jnp.bfloat16)
    return high, middle, low


def add_parts(product):
    return product[:RANK] + (product[RANK : 2 * RANK] + product[2 * RANK :])


def whole_copies(sources, targets, sems):
    return [
        pltpu.make_async_copy(source, target, sems.at[i])
        for i, (source, target) in enumerate(zip(sources, targets))
    ]


def left_kernel(
    act_hbm, grad_hbm, error_hbm, right_hbm, left_ref,
    act_ref, grad_ref, error_ref, right_ref, sems,
):
    act_copy, grad_copy, error_copy, right_copy = whole_copies(
        (act_hbm, grad_hbm, error_hbm, right_hbm),
        (act_ref, grad_ref, error_ref, right_ref),
        sems,
    )
    right_copy.start()
    grad_copy.start()
    act_copy.start()
    error_copy.start()
    right_copy.wait()
    grad_copy.wait()
    inner = jnp.dot(right_ref[...], grad_ref[...], preferred_element_type=jnp.float32)
    parts = jnp.concatenate(split(inner), axis=0)
    act_copy.wait()
    total = add_parts(jnp.dot(parts, act_ref[...], preferred_element_type=jnp.float32))
    error_copy.wait()
    total = total + jnp.dot(right_ref[...], error_ref[...], preferred_element_type=jnp.float32)
    for tile in range(ROW_TILES):
        left_ref[pl.ds(tile * RANK, RANK), :] = total[:, tile * LANES : (tile + 1) * LANES]


def left_term(act, grad, error, right):
    return pl.pallas_call(
        left_kernel,
        in_specs=[ANY] * 4,
        out_specs=WHOLE,
        out_shape=jax.ShapeDtypeStruct((ROW_TILES * RANK, LANES), jnp.float32),
        scratch_shapes=[
            pltpu.VMEM((TOK, ROWS), jnp.bfloat16),
            pltpu.VMEM((COLS, TOK), jnp.bfloat16),
            pltpu.VMEM((COLS, ROWS), jnp.bfloat16),
            pltpu.VMEM((RANK, COLS), jnp.bfloat16),
            pltpu.SemaphoreType.DMA((4,)),
        ],
        compiler_params=params(LEFT_LIMIT),
        cost_estimate=pl.CostEstimate(
            flops=2 * RANK * (COLS * (ROWS + TOK) + ROWS * TOK),
            bytes_accessed=9_000_000, transcendentals=0,
        ),
        name="left_term",
    )(act, grad, error, right)


def accumulate_kernel(
    half, act_hbm, grad_hbm, error_hbm, acc_ref,
    act_ref, grad_ref, error_ref, sems, grad_sems, error_sems,
):
    chunks = [(i, a, n) for i, (h, a, n) in enumerate(c for c in CHUNKS if c[0] == half)]
    act_copy = pltpu.make_async_copy(act_hbm, act_ref, sems.at[0])
    grad_copies, error_copies = [], []
    act_copy.start()
    for i, a, n in chunks:
        here, there = pl.ds(a, n), pl.ds(half * HALF + a, n)
        grad_copies.append(
            pltpu.make_async_copy(grad_hbm.at[there], grad_ref.at[here], grad_sems.at[i])
        )
        error_copies.append(
            pltpu.make_async_copy(error_hbm.at[there], error_ref.at[here], error_sems.at[i])
        )
        grad_copies[i].start()
        error_copies[i].start()
    act_copy.wait()
    for i, a, n in chunks:
        rows = pl.ds(a, n)
        grad_copies[i].wait()
        gradient = jnp.dot(grad_ref[rows, :], act_ref[...], preferred_element_type=jnp.float32)
        error_copies[i].wait()
        acc_ref[rows, :] = (error_ref[rows, :].astype(jnp.float32) + gradient).astype(jnp.bfloat16)


def accumulate(half, act, grad, error):
    size = HALVES[half]
    return pl.pallas_call(
        functools.partial(accumulate_kernel, half),
        in_specs=[ANY] * 3,
        out_specs=WHOLE,
        out_shape=jax.ShapeDtypeStruct((size, ROWS), jnp.bfloat16),
        scratch_shapes=[
            pltpu.VMEM((TOK, ROWS), jnp.bfloat16),
            pltpu.VMEM((size, TOK), jnp.bfloat16),
            pltpu.VMEM((size, ROWS), jnp.bfloat16),
            pltpu.SemaphoreType.DMA((1,)),
            pltpu.SemaphoreType.DMA((2,)),
            pltpu.SemaphoreType.DMA((2,)),
        ],
        compiler_params=params(ACC_LIMIT),
        cost_estimate=pl.CostEstimate(
            flops=2 * size * ROWS * TOK, bytes_accessed=8_000_000, transcendentals=0
        ),
        name="accumulate",
    )(act, grad, error)


def project_kernel(left_ref, acc_a, acc_b, out_ref, parts_ref):
    acc = (acc_a, acc_b)
    for tile in range(ROW_TILES):
        lanes = pl.ds(tile * LANES, LANES)
        mean = left_ref[pl.ds(tile * RANK, RANK), :] * (1.0 / N_DP)
        for i, part in enumerate(split(mean)):
            parts_ref[pl.ds(i * RANK, RANK), lanes] = part
    parts = parts_ref[...]
    for i, (h, a, n) in enumerate(CHUNKS):
        product = lax.dot_general(
            parts, acc[h][pl.ds(a, n), :], (((1,), (1,)), ((), ())),
            preferred_element_type=jnp.float32,
        )
        total = add_parts(product)
        for tile in range(-(-n // LANES)):
            piece = total[:, tile * LANES : min(n, (tile + 1) * LANES)]
            spare = LANES - piece.shape[1]
            if spare:
                piece = jnp.concatenate([piece, jnp.zeros((RANK, spare), jnp.float32)], axis=1)
            out_ref[pl.ds(((h * HALF + a) // LANES + tile) * RANK, RANK), :] = piece


def project(left_sum, acc_a, acc_b):
    return pl.pallas_call(
        project_kernel,
        in_specs=[WHOLE] * 3,
        out_specs=WHOLE,
        out_shape=jax.ShapeDtypeStruct((COL_TILES * RANK, LANES), jnp.float32),
        scratch_shapes=[pltpu.VMEM((3 * RANK, ROWS), jnp.bfloat16)],
        compiler_params=params(32 * 2**20),
        cost_estimate=pl.CostEstimate(
            flops=6 * COLS * ROWS * RANK, bytes_accessed=4_500_000, transcendentals=0
        ),
        name="project",
    )(left_sum, acc_a, acc_b)


def eliminate(gram):
    row = lax.broadcasted_iota(jnp.int32, (RANK, 2 * RANK), 0)
    lane = lax.broadcasted_iota(jnp.int32, (RANK, 2 * RANK), 1)
    unit = jnp.where(lane == row + RANK, 1.0, 0.0)
    work = jnp.where(lane < RANK, jnp.concatenate([gram, gram], axis=1), unit)
    for start in range(0, RANK, PIVOTS):
        columns = [
            jnp.broadcast_to(work[:, start + j : start + j + 1], (RANK, 2 * RANK))
            for j in range(PIVOTS)
        ]
        rows = [work[start + j : start + j + 1, :] for j in range(PIVOTS)]
        square = [
            [columns[m][start + j : start + j + 1, :] for m in range(PIVOTS)]
            for j in range(PIVOTS)
        ]
        update = None
        for j in range(PIVOTS):
            scale = 1.0 / square[j][j]
            for i in range(j + 1, PIVOTS):
                factor = square[i][j] * scale
                rows[i] = rows[i] - factor * rows[j]
                for m in range(j + 1, PIVOTS):
                    square[i][m] = square[i][m] - factor * square[j][m]
            factor = columns[j] * scale
            for m in range(j + 1, PIVOTS):
                columns[m] = columns[m] - factor * square[j][m]
            term = factor * rows[j]
            update = term if update is None else update + term
        work = jnp.where(row >= start + PIVOTS, work - update, work)
        for j in range(PIVOTS):
            done = rows[j] * (1.0 / jnp.sqrt(square[j][j]))
            work = jnp.where(row == start + j, done, work)
    return work[:, RANK:]


def orthonormal_kernel(left_ref, inverse_ref, out_ref):
    mean = jnp.concatenate(
        [left_ref[pl.ds(tile * RANK, RANK), :] for tile in range(ROW_TILES)], axis=1
    ) * (1.0 / N_DP)
    gram = lax.dot_general(
        mean, mean, (((1,), (1,)), ((), ())),
        precision=HIGHEST, preferred_element_type=jnp.float32,
    )
    inverse = eliminate(gram)
    inverse_ref[...] = inverse
    out_ref[...] = jnp.dot(inverse, mean, precision=HIGHEST, preferred_element_type=jnp.float32)


def orthonormal(left_sum):
    return pl.pallas_call(
        orthonormal_kernel,
        in_specs=[WHOLE],
        out_specs=[WHOLE, WHOLE],
        out_shape=[
            jax.ShapeDtypeStruct((RANK, RANK), jnp.float32),
            jax.ShapeDtypeStruct((RANK, ROWS), jnp.float32),
        ],
        compiler_params=params(16 * 2**20),
        cost_estimate=pl.CostEstimate(
            flops=40_000_000, bytes_accessed=600_000, transcendentals=0
        ),
        name="orthonormal",
    )(left_sum)


def finish_kernel(
    sum_ref, inverse_ref, left_ref, acc_a, acc_b, left_hbm, right_hbm, error_hbm,
    right_ref, error_ref, out_sems, error_sems,
):
    acc = (acc_a, acc_b)
    starts = [h * HALF + a for h, a, n in CHUNKS]
    error_copies = [
        pltpu.make_async_copy(
            error_ref.at[pl.ds(start, chunk[2])],
            error_hbm.at[pl.ds(start, chunk[2])],
            error_sems.at[i],
        )
        for i, (start, chunk) in enumerate(zip(starts, CHUNKS))
    ]
    left_copy = pltpu.make_async_copy(left_ref, left_hbm, out_sems.at[0])
    right_copy = pltpu.make_async_copy(right_ref, right_hbm, out_sems.at[1])
    terms = jnp.concatenate(
        [sum_ref[pl.ds(tile * RANK, RANK), :] for tile in range(COL_TILES)], axis=1
    )
    right = jnp.dot(
        inverse_ref[...], terms, precision=HIGHEST, preferred_element_type=jnp.float32
    )
    right = (right * (1.0 / N_DP)).astype(jnp.bfloat16)
    right_ref[...] = right[:, :COLS]
    left_copy.start()
    right_copy.start()
    left = left_ref[...].astype(jnp.bfloat16)
    for i, (h, a, n) in enumerate(CHUNKS):
        start = starts[i]
        update = lax.dot_general(
            right_ref[:, start : start + n], left, (((0,), (0,)), ((), ())),
            preferred_element_type=jnp.float32,
        )
        held = acc[h][pl.ds(a, n), :].astype(jnp.float32)
        error_ref[pl.ds(start, n), :] = (held - update).astype(jnp.bfloat16)
        error_copies[i].start()
    left_copy.wait()
    right_copy.wait()
    for copy in error_copies:
        copy.wait()


def finish(right_sum, inverse, left, acc_a, acc_b):
    return pl.pallas_call(
        finish_kernel,
        in_specs=[WHOLE] * 5,
        out_specs=[ANY, ANY, ANY],
        out_shape=[
            jax.ShapeDtypeStruct((RANK, ROWS), jnp.float32),
            jax.ShapeDtypeStruct((RANK, COLS), jnp.bfloat16),
            jax.ShapeDtypeStruct((COLS, ROWS), jnp.bfloat16),
        ],
        scratch_shapes=[
            pltpu.VMEM((RANK, COLS), jnp.bfloat16),
            pltpu.VMEM((COLS, ROWS), jnp.bfloat16),
            pltpu.SemaphoreType.DMA((2,)),
            pltpu.SemaphoreType.DMA((len(CHUNKS),)),
        ],
        compiler_params=params(32 * 2**20),
        cost_estimate=pl.CostEstimate(
            flops=2 * COLS * ROWS * RANK, bytes_accessed=8_500_000, transcendentals=0
        ),
        name="finish",
    )(right_sum, inverse, left, acc_a, acc_b)


def exchange(pieces, axes):
    return lax.all_to_all(pieces, axes, 0, 0, tiled=True)


def spread(total, count):
    return jnp.broadcast_to(total[None], (count,) + total.shape)


def sum_left(part, first, second):
    mine = jnp.sum(exchange(part.reshape(32, 16, LANES), PLANE), axis=0)
    mine, first = lax.optimization_barrier((mine, first))
    mine = jnp.sum(exchange(spread(mine, 8), Z), axis=0)
    total = exchange(spread(mine, 32), PLANE).reshape(part.shape)
    return total, (first, second)


def sum_right(part, work):
    mine = jnp.sum(exchange(part.reshape(8, 120, LANES), NEAR), axis=0)
    mine, work = lax.optimization_barrier((mine, work))
    mine = jnp.sum(exchange(spread(mine, 4), "zh"), axis=0)
    return exchange(spread(mine, 8), NEAR).reshape(part.shape), work


def local(activations, output_grads, error_buffer, right_start):
    grad, error = output_grads.T, error_buffer[0].T
    left_part = left_term(activations, grad, error, right_start.T)
    acc = [accumulate(half, activations, grad, error) for half in range(2)]
    left_sum, acc = sum_left(left_part, *acc)
    right_part = project(left_sum, *acc)
    right_sum, (inverse, left) = sum_right(right_part, orthonormal(left_sum))
    left_factor, right_factor, new_error = finish(right_sum, inverse, left, *acc)
    return (left_factor.T, right_factor.T, new_error.T[None])


def solution(mesh):
    fine = Mesh(mesh.devices.reshape(4, 4, 2, 4, 2), DP + ("y", "core"))
    tensor = ("y", "core")
    return jax.shard_map(
        local,
        mesh=fine,
        in_specs=(P(DP, None), P(DP, tensor), P(DP, None, tensor), P(tensor, None)),
        out_specs=(P(), P(tensor, None), P(DP, None, tensor)),
        check_vma=False,
    )
```

time: 108 us -> 99 us (0.917)
  blocking collectives: 13.3 us -> 40.1 us
  waiting for transfers between devices: 24.8 us -> 12.2 us
  other arithmetic: 12.3 us -> 0.09 us
  starting transfers between devices: 27.3 us -> 16.3 us
  local copies, waits for them, and re-layouts: 1.63 us -> 7.84 us
  Pallas kernels: 25.9 us -> 21 us
  matrix products: 1.65 us -> 0 us
    all_to_all x1 -> x3, blocking collectives: 13.3 us -> 40.1 us  [exchange(): return lax.all_to_all(pieces, axes, 0, 0, tiled=True)]
    all_to_all x4 -> x3, waiting for transfers between devices: 24.8 us -> 12.2 us  [exchange(): return lax.all_to_all(pieces, axes, 0, 0, tiled=True)]
    another operation x5 -> x0, other arithmetic: 12.1 us -> none  [the longest x3 6.52 us: orthonormal(): lower = jnp.linalg.cholesky(gram)]
    all_to_all x4 -> x3, starting transfers between devices: 27.3 us -> 16.3 us  [exchange(): return lax.all_to_all(pieces, axes, 0, 0, tiled=True)]
    unnamed x0 -> x10, local copies, waits for them, and re-layouts: none -> 7.06 us
    pallas_call x2, Pallas kernels: 11.4 us -> 7.91 us  [accumulate(): pl.pallas_call(functools.partial(accumulate_kernel, half), in_specs=[ANY]...]
    dot_general x2 -> x0, matrix products: 1.42 us -> none  [the longest x1 1.06 us: orthonormal(): return (inverse, jnp.dot(inverse, mean, precision=HIGHEST))]
    pallas_call x2 -> x3, Pallas kernels: 9.16 us -> 7.84 us  [the longest x1 2.87 us: orthonormal(): pl.pallas_call(orthonormal_kernel, in_specs=[WHOLE], out_specs=[WHOLE, WH...]
  transfers between devices with their start and end apart: 4 -> 3, of which waited for: 4 -> 3; matrix products, arithmetic and copies ran while one was open for 13% -> 0% of each run, Pallas kernels for 11% -> 11%
where the time goes in v3:
time: 99 us; the launch traced here: 98.4 us
  blocking collectives  40.1 us (41%)
  Pallas kernels  21 us (21%)
  starting transfers between devices  16.3 us (16%)
  waiting for transfers between devices  12.2 us (12%)
  local copies, waits for them, and re-layouts  7.84 us (8%)
    all_to_all x3, blocking collectives, exchange(): return lax.all_to_all(pieces, axes, 0, 0, tiled=True)  40.1 us
    all_to_all x3, starting transfers between devices, exchange(): return lax.all_to_all(pieces, axes, 0, 0, tiled=True)  16.3 us
    all_to_all x3, waiting for transfers between devices, exchange(): return lax.all_to_all(pieces, axes, 0, 0, tiled=True)  12.2 us
    pallas_call x2, Pallas kernels, accumulate(): pl.pallas_call(functools.partial(accumulate_kernel, half), in_specs=[ANY]...  7.91 us
    unnamed x10, local copies, waits for them, and re-layouts  7.06 us
    pallas_call x1, Pallas kernels, left_term(): pl.pallas_call(left_kernel, in_specs=[ANY] * 4, out_specs=WHOLE, out_shap...  5.29 us
    pallas_call x1, Pallas kernels, orthonormal(): pl.pallas_call(orthonormal_kernel, in_specs=[WHOLE], out_specs=[WHOLE, WH...  2.87 us
    pallas_call x1, Pallas kernels, finish(): pl.pallas_call(finish_kernel, in_specs=[WHOLE] * 5, out_specs=[ANY, ANY,...  2.74 us
  transfers between devices with their start and end apart: 3, of which 3 were waited for; matrix products, arithmetic and copies ran while one was open for 0% of the time, Pallas kernels for 11%

profile of v3, /device:TPU:32, one launch (start us, length us, event | category | flops | bytes accessed | tf_op | source)
XLA Modules:
  0.0 98.4 jit_solution(6061996688211148553)
XLA Ops:
  0.6 5.3 %left_term.1 = f32[512,128]{1,0:T(8,128)} custom-call(bf16[896,1024]{1,0:T(8,128)(2,1)} %act_hbm.5, bf16[1848,896]{1,0:T(8,128)(2,1)} %bitcast.20, bf16[1848,1024]{1,0:T(8,128)(2,1)} %bitcast.17, bf16[64,1848]{1,0:T(8,128)(2,1)} %bitcast.24), custom_call_target="tpu_custom_call" | custom-call | flops 571604992 | bytes 9000000 | tf_op jit(solution)/shard_map/left_term/pallas_call | solution.py:79
  5.9 7.3 %all-to-all-start = ((f32[32,16,128]{2,1,0:T(8,128)}), f32[32,16,128]{2,1,0:T(8,128)S(1)}, u32[]{:S(2)}, u32[]{:S(2)}) async-start(f32[32,16,128]{2,1,0:T(8,128)} %bitcast.23), calls=%async_computation | async-start | bytes 524288 | tf_op jit(solution)/shard_map/all_to_all | solution.py:319
  13.3 0.0 copy-start
  13.3 1.5 %copy-done = bf16[896,1024]{1,0:T(8,128)(2,1)S(1)} copy-done((bf16[896,1024]{1,0:T(8,128)(2,1)S(1)}, bf16[896,1024]{1,0:T(8,128)(2,1)}, u32[]{:S(2)}) %copy-start) | copy-done | bytes 1835032
  14.8 4.2 %accumulate.2.acc_a = bf16[1024,1024]{1,0:T(8,128)(2,1)S(1)} custom-call(bf16[896,1024]{1,0:T(8,128)(2,1)S(1)} %copy-done, bf16[1848,896]{1,0:T(8,128)(2,1)} %bitcast.21, bf16[1848,1024]{1,0:T(8,128)(2,1)} %bitcast.18), custom_call_target="tpu_custom_call" | custom-call | flops 1879048192 | bytes 8000000 | tf_op jit(solution)/shard_map/accumulate/pallas_call | solution.py:129
  19.0 3.2 %all-to-all-done = f32[32,16,128]{2,1,0:T(8,128)S(1)} async-done(((f32[32,16,128]{2,1,0:T(8,128)}), f32[32,16,128]{2,1,0:T(8,128)S(1)}, u32[]{:S(2)}, u32[]{:S(2)}) %all-to-all-start) | async-done | bytes 262176 | tf_op jit(solution)/shard_map/all_to_all | solution.py:319
  22.3 15.3 %all_to_all.30 = f32[8,16,128]{2,1,0:T(8,128)S(1)} all-to-all(f32[8,16,128]{2,1,0:T(8,128)S(1)} %broadcast_in_dim.10), channel_id=1, replica_groups=mesh['x'=4,'zh'=4,'zl'=2,'y'=4,'core'=2] {'zh','zl'}, dimensions={0} | all-to-all | bytes 131072 | tf_op jit(solution)/shard_map/all_to_all | solution.py:319
  37.6 0.7 broadcast_in_dim.11
  38.3 4.2 %all-to-all-start.2 = ((f32[32,16,128]{2,1,0:T(8,128)}), f32[32,16,128]{2,1,0:T(8,128)S(1)}, u32[]{:S(2)}, u32[]{:S(2)}) async-start(f32[32,16,128]{2,1,0:T(8,128)} %broadcast_in_dim.11), calls=%async_computation.2 | async-start | bytes 524288 | tf_op jit(solution)/shard_map/all_to_all | solution.py:319
  42.5 0.0 copy-start.1
  42.5 1.5 %copy-done.1 = bf16[896,1024]{1,0:T(8,128)(2,1)S(1)} copy-done((bf16[896,1024]{1,0:T(8,128)(2,1)S(1)}, bf16[896,1024]{1,0:T(8,128)(2,1)}, u32[]{:S(2)}) %copy-start.1) | copy-done | bytes 1835032
  44.0 3.7 %accumulate.3.acc_b = bf16[824,1024]{1,0:T(8,128)(2,1)S(1)} custom-call(bf16[896,1024]{1,0:T(8,128)(2,1)S(1)} %copy-done.1, bf16[1848,896]{1,0:T(8,128)(2,1)} %bitcast.22, bf16[1848,1024]{1,0:T(8,128)(2,1)} %bitcast.19), custom_call_target="tpu_custom_call" | custom-call | flops 1512046592 | bytes 8000000 | tf_op jit(solution)/shard_map/accumulate/pallas_call | solution.py:129
  47.7 0.0 copy-start.2
  47.7 1.2 %copy-done.2 = bf16[824,1024]{1,0:T(8,128)(2,1)} copy-done((bf16[824,1024]{1,0:T(8,128)(2,1)}, bf16[824,1024]{1,0:T(8,128)(2,1)S(1)}, u32[]{:S(2)}) %copy-start.2) | copy-done | bytes 1687576
  48.9 2.5 %all-to-all-done.2 = f32[32,16,128]{2,1,0:T(8,128)S(1)} async-done(((f32[32,16,128]{2,1,0:T(8,128)}), f32[32,16,128]{2,1,0:T(8,128)S(1)}, u32[]{:S(2)}, u32[]{:S(2)}) %all-to-all-start.2) | async-done | bytes 262176 | tf_op jit(solution)/shard_map/all_to_all | solution.py:319
  51.4 0.0 copy-start.3
  51.4 1.4 %copy-done.3 = bf16[824,1024]{1,0:T(8,128)(2,1)S(1)} copy-done((bf16[824,1024]{1,0:T(8,128)(2,1)S(1)}, bf16[824,1024]{1,0:T(8,128)(2,1)}, u32[]{:S(2)}) %copy-start.3) | copy-done | bytes 1687576
  52.8 2.2 %project.1 = f32[960,128]{1,0:T(8,128)} custom-call(f32[512,128]{1,0:T(8,128)S(1)} %bitcast.14, bf16[1024,1024]{1,0:T(8,128)(2,1)S(1)} %accumulate.2.acc_a, bf16[824,1024]{1,0:T(8,128)(2,1)S(1)} %copy-done.3), custom_call_target="tpu_custom_call" | custom-call | flops 726663168 | bytes 4500000 | tf_op jit(solution)/shard_map/project/pallas_call | solution.py:173
  55.1 4.8 %all-to-all-start.3 = ((f32[8,120,128]{2,1,0:T(8,128)}), f32[8,120,128]{2,1,0:T(8,128)S(1)}, u32[]{:S(2)}, u32[]{:S(2)}) async-start(f32[8,120,128]{2,1,0:T(8,128)} %bitcast.7), calls=%async_computation.3 | async-start | bytes 983040 | tf_op jit(solution)/shard_map/all_to_all | solution.py:319
  59.9 2.9 %orthonormal.1 = (f32[64,64]{1,0:T(8,128)S(1)}, f32[64,1024]{1,0:T(8,128)S(1)}) custom-call(f32[512,128]{1,0:T(8,128)S(1)} %bitcast.15), custom_call_target="tpu_custom_call" | custom-call | flops 40000000 | bytes 600000 | tf_op jit(solution)/shard_map/orthonormal/pallas_call | solution.py:236
  62.8 6.5 %all-to-all-done.3 = f32[8,120,128]{2,1,0:T(8,128)S(1)} async-done(((f32[8,120,128]{2,1,0:T(8,128)}), f32[8,120,128]{2,1,0:T(8,128)S(1)}, u32[]{:S(2)}, u32[]{:S(2)}) %all-to-all-start.3) | async-done | bytes 491552 | tf_op jit(solution)/shard_map/all_to_all | solution.py:319
  69.3 13.1 %all_to_all.31 = f32[4,120,128]{2,1,0:T(8,128)S(1)} all-to-all(f32[4,120,128]{2,1,0:T(8,128)S(1)} %broadcast_in_dim.12), channel_id=1, replica_groups=mesh['x'=4,'zh'=4,'zl'=2,'y'=4,'core'=2] {'zh'}, dimensions={0} | all-to-all | bytes 491520 | tf_op jit(solution)/shard_map/all_to_all | solution.py:319
  82.5 11.7 %all_to_all.32 = f32[8,120,128]{2,1,0:T(8,128)S(1)} all-to-all(f32[8,120,128]{2,1,0:T(8,128)S(1)} %broadcast_in_dim.13), channel_id=1, replica_groups=mesh['x'=4,'zh'=4,'zl'=2,'y'=4,'core'=2] {'x','zl'}, dimensions={0} | all-to-all | bytes 983040 | tf_op jit(solution)/shard_map/all_to_all | solution.py:319
  94.2 0.0 copy-start.4
  94.2 1.4 %copy-done.4 = bf16[824,1024]{1,0:T(8,128)(2,1)S(1)} copy-done((bf16[824,1024]{1,0:T(8,128)(2,1)S(1)}, bf16[824,1024]{1,0:T(8,128)(2,1)}, u32[]{:S(2)}) %copy-start.4) | copy-done | bytes 1687576
  95.6 2.7 %finish.1 = (f32[64,1024]{1,0:T(8,128)}, bf16[64,1848]{1,0:T(8,128)(2,1)}, bf16[1848,1024]{1,0:T(8,128)(2,1)}) custom-call(f32[960,128]{1,0:T(8,128)S(1)} %bitcast.16, f32[64,64]{1,0:T(8,128)S(1)} %get-tuple-element.18.inverse_ref, f32[64,1024]{1,0:T(8,128)S(1)} %get-tuple-element.19.left_ref, bf16[1024,1024]{1,0:T(8,128)(2,1)S(1)} %accumulate.2.acc_a, ...), custom_call_target="tpu_custom_call" | custom-call | flops 242221056 | bytes 8500000 | tf_op jit(solution)/shard_map/finish/pallas_call | solution.py:295
  (7 shorter events, 0.1 us)
Async XLA Ops:
  5.9 16.3 %all-to-all-start = ((f32[32,16,128]{2,1,0:T(8,128)}), f32[32,16,128]{2,1,0:T(8,128)S(1)}, u32[]{:S(2)}, u32[]{:S(2)}) async-start(f32[32,16,128]{2,1,0:T(8,128)} %bitcast.23), calls=%async_computation | async-start | bytes 524288 | tf_op jit(solution)/shard_map/all_to_all | solution.py:319
  13.3 1.5 %copy-start = (bf16[896,1024]{1,0:T(8,128)(2,1)S(1)}, bf16[896,1024]{1,0:T(8,128)(2,1)}, u32[]{:S(2)}) copy-start(bf16[896,1024]{1,0:T(8,128)(2,1)} %act_hbm.5) | copy-start | bytes 5505028
  38.3 13.1 %all-to-all-start.2 = ((f32[32,16,128]{2,1,0:T(8,128)}), f32[32,16,128]{2,1,0:T(8,128)S(1)}, u32[]{:S(2)}, u32[]{:S(2)}) async-start(f32[32,16,128]{2,1,0:T(8,128)} %broadcast_in_dim.11), calls=%async_computation.2 | async-start | bytes 524288 | tf_op jit(solution)/shard_map/all_to_all | solution.py:319
  42.5 1.5 %copy-start.1 = (bf16[896,1024]{1,0:T(8,128)(2,1)S(1)}, bf16[896,1024]{1,0:T(8,128)(2,1)}, u32[]{:S(2)}) copy-start(bf16[896,1024]{1,0:T(8,128)(2,1)} %act_hbm.5) | copy-start | bytes 5505028
  47.7 1.2 %copy-start.2 = (bf16[824,1024]{1,0:T(8,128)(2,1)}, bf16[824,1024]{1,0:T(8,128)(2,1)S(1)}, u32[]{:S(2)}) copy-start(bf16[824,1024]{1,0:T(8,128)(2,1)S(1)} %accumulate.3.acc_b) | copy-start | bytes 5062660
  51.4 1.4 %copy-start.3 = (bf16[824,1024]{1,0:T(8,128)(2,1)S(1)}, bf16[824,1024]{1,0:T(8,128)(2,1)}, u32[]{:S(2)}) copy-start(bf16[824,1024]{1,0:T(8,128)(2,1)} %copy-done.2) | copy-start | bytes 5062660
  55.1 14.2 %all-to-all-start.3 = ((f32[8,120,128]{2,1,0:T(8,128)}), f32[8,120,128]{2,1,0:T(8,128)S(1)}, u32[]{:S(2)}, u32[]{:S(2)}) async-start(f32[8,120,128]{2,1,0:T(8,128)} %bitcast.7), calls=%async_computation.3 | async-start | bytes 983040 | tf_op jit(solution)/shard_map/all_to_all | solution.py:319
  94.2 1.4 %copy-start.4 = (bf16[824,1024]{1,0:T(8,128)(2,1)S(1)}, bf16[824,1024]{1,0:T(8,128)(2,1)}, u32[]{:S(2)}) copy-start(bf16[824,1024]{1,0:T(8,128)(2,1)} %copy-done.2) | copy-start | bytes 5062660

commit v4 on v3

--- a/solution.py
+++ b/solution.py
@@ -11,16 +11,17 @@
 LANES = 128
 ROW_TILES = ROWS // LANES
 COL_TILES = -(-COLS // LANES)
-HALF = 1024
+HALF = 640
 HALVES = (HALF, COLS - HALF)
-CHUNKS = ((0, 0, 512), (0, 512, 512), (1, 0, 512), (1, 512, COLS - HALF - 512))
+SPARE_ROWS = 12288
+CHUNKS = ((1, 0, 640), (1, 640, COLS - HALF - 640), (0, 0, 384), (0, 384, HALF - 384))
 Z = ("zh", "zl")
 DP = ("x",) + Z
 NEAR = ("x", "zl")
 PLANE = ("x", "y", "core")
-VMEM_LIMIT = 53 * 2**20
+VMEM_LIMIT = 32 * 2**20
 LEFT_LIMIT = 56 * 2**20
-ACC_LIMIT = 49 * 2**20
+ACC_LIMITS = (56 * 2**20, 49 * 2**20 + 2**19)
 HIGHEST = lax.Precision.HIGHEST
 PIVOTS = 8
 ANY = pl.BlockSpec(memory_space=pl.ANY)
@@ -98,12 +99,13 @@
 
 
 def accumulate_kernel(
-    half, act_hbm, grad_hbm, error_hbm, acc_ref,
-    act_ref, grad_ref, error_ref, sems, grad_sems, error_sems,
+    half, act_hbm, grad_hbm, error_hbm, out_ref,
+    act_ref, grad_ref, error_ref, sems, grad_sems, error_sems, *spare
 ):
     chunks = [(i, a, n) for i, (h, a, n) in enumerate(c for c in CHUNKS if c[0] == half)]
     act_copy = pltpu.make_async_copy(act_hbm, act_ref, sems.at[0])
-    grad_copies, error_copies = [], []
+    grad_copies, error_copies, acc_copies = [], [], []
+    acc_ref = spare[0] if spare else out_ref
     act_copy.start()
     for i, a, n in chunks:
         here, there = pl.ds(a, n), pl.ds(half * HALF + a, n)
@@ -113,6 +115,10 @@
         error_copies.append(
             pltpu.make_async_copy(error_hbm.at[there], error_ref.at[here], error_sems.at[i])
         )
+        if spare:
+            acc_copies.append(
+                pltpu.make_async_copy(acc_ref.at[here], out_ref.at[here], spare[1].at[i])
+            )
         grad_copies[i].start()
         error_copies[i].start()
     act_copy.wait()
@@ -122,15 +128,20 @@
         gradient = jnp.dot(grad_ref[rows, :], act_ref[...], preferred_element_type=jnp.float32)
         error_copies[i].wait()
         acc_ref[rows, :] = (error_ref[rows, :].astype(jnp.float32) + gradient).astype(jnp.bfloat16)
+        if spare:
+            acc_copies[i].start()
+    for copy in acc_copies:
+        copy.wait()
 
 
 def accumulate(half, act, grad, error):
     size = HALVES[half]
+    spare = [pltpu.VMEM((size, ROWS), jnp.bfloat16), pltpu.SemaphoreType.DMA((2,))]
     return pl.pallas_call(
         functools.partial(accumulate_kernel, half),
         in_specs=[ANY] * 3,
-        out_specs=WHOLE,
-        out_shape=jax.ShapeDtypeStruct((size, ROWS), jnp.bfloat16),
+        out_specs=WHOLE if half else ANY,
+        out_shape=jax.ShapeDtypeStruct((size if half else SPARE_ROWS, ROWS), jnp.bfloat16),
         scratch_shapes=[
             pltpu.VMEM((TOK, ROWS), jnp.bfloat16),
             pltpu.VMEM((size, TOK), jnp.bfloat16),
@@ -138,8 +149,9 @@
             pltpu.SemaphoreType.DMA((1,)),
             pltpu.SemaphoreType.DMA((2,)),
             pltpu.SemaphoreType.DMA((2,)),
-        ],
-        compiler_params=params(ACC_LIMIT),
+        ]
+        + spare * (1 - half),
+        compiler_params=params(ACC_LIMITS[half]),
         cost_estimate=pl.CostEstimate(
             flops=2 * size * ROWS * TOK, bytes_accessed=8_000_000, transcendentals=0
         ),
@@ -147,8 +159,19 @@
     )(act, grad, error)
 
 
-def project_kernel(left_ref, acc_a, acc_b, out_ref, parts_ref):
-    acc = (acc_a, acc_b)
+def first_half(source, target, sems):
+    return {
+        i: pltpu.make_async_copy(source.at[pl.ds(a, n)], target.at[pl.ds(a, n)], sems.at[i])
+        for i, (h, a, n) in enumerate(CHUNKS)
+        if h == 0
+    }
+
+
+def project_kernel(left_ref, acc_a, acc_b, out_ref, parts_ref, half_a, sems):
+    acc = (half_a, acc_b)
+    copies = first_half(acc_a, half_a, sems)
+    for copy in copies.values():
+        copy.start()
     for tile in range(ROW_TILES):
         lanes = pl.ds(tile * LANES, LANES)
         mean = left_ref[pl.ds(tile * RANK, RANK), :] * (1.0 / N_DP)
@@ -156,6 +179,8 @@
             parts_ref[pl.ds(i * RANK, RANK), lanes] = part
     parts = parts_ref[...]
     for i, (h, a, n) in enumerate(CHUNKS):
+        if i in copies:
+            copies[i].wait()
         product = lax.dot_general(
             parts, acc[h][pl.ds(a, n), :], (((1,), (1,)), ((), ())),
             preferred_element_type=jnp.float32,
@@ -172,11 +197,15 @@
 def project(left_sum, acc_a, acc_b):
     return pl.pallas_call(
         project_kernel,
-        in_specs=[WHOLE] * 3,
+        in_specs=[WHOLE, ANY, WHOLE],
         out_specs=WHOLE,
         out_shape=jax.ShapeDtypeStruct((COL_TILES * RANK, LANES), jnp.float32),
-        scratch_shapes=[pltpu.VMEM((3 * RANK, ROWS), jnp.bfloat16)],
-        compiler_params=params(32 * 2**20),
+        scratch_shapes=[
+            pltpu.VMEM((3 * RANK, ROWS), jnp.bfloat16),
+            pltpu.VMEM((HALVES[0], ROWS), jnp.bfloat16),
+            pltpu.SemaphoreType.DMA((len(CHUNKS),)),
+        ],
+        compiler_params=params(),
         cost_estimate=pl.CostEstimate(
             flops=6 * COLS * ROWS * RANK, bytes_accessed=4_500_000, transcendentals=0
         ),
@@ -251,9 +280,12 @@
 
 def finish_kernel(
     sum_ref, inverse_ref, left_ref, acc_a, acc_b, left_hbm, right_hbm, error_hbm,
-    right_ref, error_ref, out_sems, error_sems,
+    half_a, right_ref, error_ref, sems, out_sems, error_sems,
 ):
-    acc = (acc_a, acc_b)
+    acc = (half_a, acc_b)
+    copies = first_half(acc_a, half_a, sems)
+    for copy in copies.values():
+        copy.start()
     starts = [h * HALF + a for h, a, n in CHUNKS]
     error_copies = [
         pltpu.make_async_copy(
@@ -282,6 +314,8 @@
             right_ref[:, start : start + n], left, (((0,), (0,)), ((), ())),
             preferred_element_type=jnp.float32,
         )
+        if i in copies:
+            copies[i].wait()
         held = acc[h][pl.ds(a, n), :].astype(jnp.float32)
         error_ref[pl.ds(start, n), :] = (held - update).astype(jnp.bfloat16)
         error_copies[i].start()
@@ -294,7 +328,7 @@
 def finish(right_sum, inverse, left, acc_a, acc_b):
     return pl.pallas_call(
         finish_kernel,
-        in_specs=[WHOLE] * 5,
+        in_specs=[WHOLE] * 3 + [ANY, WHOLE],
         out_specs=[ANY, ANY, ANY],
         out_shape=[
             jax.ShapeDtypeStruct((RANK, ROWS), jnp.float32),
@@ -302,12 +336,14 @@
             jax.ShapeDtypeStruct((COLS, ROWS), jnp.bfloat16),
         ],
         scratch_shapes=[
+            pltpu.VMEM((HALVES[0], ROWS), jnp.bfloat16),
             pltpu.VMEM((RANK, COLS), jnp.bfloat16),
             pltpu.VMEM((COLS, ROWS), jnp.bfloat16),
+            pltpu.SemaphoreType.DMA((len(CHUNKS),)),
             pltpu.SemaphoreType.DMA((2,)),
             pltpu.SemaphoreType.DMA((len(CHUNKS),)),
         ],
-        compiler_params=params(32 * 2**20),
+        compiler_params=params(),
         cost_estimate=pl.CostEstimate(
             flops=2 * COLS * ROWS * RANK, bytes_accessed=8_500_000, transcendentals=0
         ),

time: 99 us -> 97.6 us (0.986)
  local copies, waits for them, and re-layouts: 7.84 us -> 2.27 us
  Pallas kernels: 21 us -> 24.5 us
  waiting for transfers between devices: 12.2 us -> 13.4 us
    unnamed x10 -> x2, local copies, waits for them, and re-layouts: 7.06 us -> 1.49 us
    pallas_call x2, Pallas kernels: 4.97 us -> 6.84 us  [the longest x1 3.72 us: project(): pl.pallas_call(project_kernel, in_specs=[WHOLE, ANY, WHOLE], out_specs=WH...]
    pallas_call x2, Pallas kernels: 7.91 us -> 9.47 us  [accumulate(): pl.pallas_call(functools.partial(accumulate_kernel, half), in_specs=[ANY]...]
    all_to_all x3, waiting for transfers between devices: 12.2 us -> 13.4 us  [exchange(): return lax.all_to_all(pieces, axes, 0, 0, tiled=True)]
  transfers between devices with their start and end apart: 3 -> 3, of which waited for: 3 -> 3; matrix products, arithmetic and copies ran while one was open for 0% -> 0% of each run, Pallas kernels for 11% -> 13%
where the time goes in v4:
time: 97.6 us; the launch traced here: 97.1 us
  blocking collectives  40.1 us (41%)
  Pallas kernels  24.5 us (25%)
  starting transfers between devices  16.1 us (16%)
  waiting for transfers between devices  13.4 us (14%)
  local copies, waits for them, and re-layouts  2.27 us (2%)
    all_to_all x3, blocking collectives, exchange(): return lax.all_to_all(pieces, axes, 0, 0, tiled=True)  40.1 us
    all_to_all x3, starting transfers between devices, exchange(): return lax.all_to_all(pieces, axes, 0, 0, tiled=True)  16.1 us
    all_to_all x3, waiting for transfers between devices, exchange(): return lax.all_to_all(pieces, axes, 0, 0, tiled=True)  13.4 us
    pallas_call x2, Pallas kernels, accumulate(): pl.pallas_call(functools.partial(accumulate_kernel, half), in_specs=[ANY]...  9.47 us
    pallas_call x1, Pallas kernels, left_term(): pl.pallas_call(left_kernel, in_specs=[ANY] * 4, out_specs=WHOLE, out_shap...  5.29 us
    pallas_call x1, Pallas kernels, project(): pl.pallas_call(project_kernel, in_specs=[WHOLE, ANY, WHOLE], out_specs=WH...  3.72 us
    pallas_call x1, Pallas kernels, finish(): pl.pallas_call(finish_kernel, in_specs=[WHOLE] * 3 + [ANY, WHOLE], out_sp...  3.12 us
    pallas_call x1, Pallas kernels, orthonormal(): pl.pallas_call(orthonormal_kernel, in_specs=[WHOLE], out_specs=[WHOLE, WH...  2.87 us
  transfers between devices with their start and end apart: 3, of which 3 were waited for; matrix products, arithmetic and copies ran while one was open for 0% of the time, Pallas kernels for 13%

profile of v4, /device:TPU:32, one launch (start us, length us, event | category | flops | bytes accessed | tf_op | source)
XLA Modules:
  0.0 97.1 jit_solution(17196319105796563300)
XLA Ops:
  0.6 5.3 %left_term.1 = f32[512,128]{1,0:T(8,128)} custom-call(bf16[896,1024]{1,0:T(8,128)(2,1)} %act_hbm.5, bf16[1848,896]{1,0:T(8,128)(2,1)} %bitcast.20, bf16[1848,1024]{1,0:T(8,128)(2,1)} %bitcast.17, bf16[64,1848]{1,0:T(8,128)(2,1)} %bitcast.24), custom_call_target="tpu_custom_call" | custom-call | flops 571604992 | bytes 9000000 | tf_op jit(solution)/shard_map/left_term/pallas_call | solution.py:80
  5.9 7.3 %all-to-all-start = ((f32[32,16,128]{2,1,0:T(8,128)}), f32[32,16,128]{2,1,0:T(8,128)S(1)}, u32[]{:S(2)}, u32[]{:S(2)}) async-start(f32[32,16,128]{2,1,0:T(8,128)} %bitcast.23), calls=%async_computation | async-start | bytes 524288 | tf_op jit(solution)/shard_map/all_to_all | solution.py:355
  13.3 4.7 %accumulate.2.acc_a = bf16[12288,1024]{1,0:T(8,128)(2,1)} custom-call(bf16[896,1024]{1,0:T(8,128)(2,1)} %act_hbm.5, bf16[1848,896]{1,0:T(8,128)(2,1)} %bitcast.21, bf16[1848,1024]{1,0:T(8,128)(2,1)} %bitcast.18), custom_call_target="tpu_custom_call" | custom-call | flops 1174405120 | bytes 8000000 | tf_op jit(solution)/shard_map/accumulate/pallas_call | solution.py:140
  18.0 4.2 %all-to-all-done = f32[32,16,128]{2,1,0:T(8,128)S(1)} async-done(((f32[32,16,128]{2,1,0:T(8,128)}), f32[32,16,128]{2,1,0:T(8,128)S(1)}, u32[]{:S(2)}, u32[]{:S(2)}) %all-to-all-start) | async-done | bytes 262176 | tf_op jit(solution)/shard_map/all_to_all | solution.py:355
  22.3 15.3 %all_to_all.30 = f32[8,16,128]{2,1,0:T(8,128)S(1)} all-to-all(f32[8,16,128]{2,1,0:T(8,128)S(1)} %broadcast_in_dim.10), channel_id=1, replica_groups=mesh['x'=4,'zh'=4,'zl'=2,'y'=4,'core'=2] {'zh','zl'}, dimensions={0} | all-to-all | bytes 131072 | tf_op jit(solution)/shard_map/all_to_all | solution.py:355
  37.6 0.7 broadcast_in_dim.11
  38.3 3.9 %all-to-all-start.2 = ((f32[32,16,128]{2,1,0:T(8,128)}), f32[32,16,128]{2,1,0:T(8,128)S(1)}, u32[]{:S(2)}, u32[]{:S(2)}) async-start(f32[32,16,128]{2,1,0:T(8,128)} %broadcast_in_dim.11), calls=%async_computation.2 | async-start | bytes 524288 | tf_op jit(solution)/shard_map/all_to_all | solution.py:355
  42.2 0.0 copy-start
  42.2 1.5 %copy-done = bf16[896,1024]{1,0:T(8,128)(2,1)S(1)} copy-done((bf16[896,1024]{1,0:T(8,128)(2,1)S(1)}, bf16[896,1024]{1,0:T(8,128)(2,1)}, u32[]{:S(2)}) %copy-start) | copy-done | bytes 1835032
  43.7 4.7 %accumulate.3.acc_b = bf16[1208,1024]{1,0:T(8,128)(2,1)S(1)} custom-call(bf16[896,1024]{1,0:T(8,128)(2,1)S(1)} %copy-done, bf16[1848,896]{1,0:T(8,128)(2,1)} %bitcast.22, bf16[1848,1024]{1,0:T(8,128)(2,1)} %bitcast.19), custom_call_target="tpu_custom_call" | custom-call | flops 2216689664 | bytes 8000000 | tf_op jit(solution)/shard_map/accumulate/pallas_call | solution.py:140
  48.4 2.7 %all-to-all-done.2 = f32[32,16,128]{2,1,0:T(8,128)S(1)} async-done(((f32[32,16,128]{2,1,0:T(8,128)}), f32[32,16,128]{2,1,0:T(8,128)S(1)}, u32[]{:S(2)}, u32[]{:S(2)}) %all-to-all-start.2) | async-done | bytes 262176 | tf_op jit(solution)/shard_map/all_to_all | solution.py:355
  51.1 3.7 %project.1 = f32[960,128]{1,0:T(8,128)} custom-call(f32[512,128]{1,0:T(8,128)S(1)} %bitcast.14, bf16[12288,1024]{1,0:T(8,128)(2,1)} %accumulate.2.acc_a, bf16[1208,1024]{1,0:T(8,128)(2,1)S(1)} %accumulate.3.acc_b), custom_call_target="tpu_custom_call" | custom-call | flops 726663168 | bytes 4500000 | tf_op jit(solution)/shard_map/project/pallas_call | solution.py:198
  54.8 4.9 %all-to-all-start.3 = ((f32[8,120,128]{2,1,0:T(8,128)}), f32[8,120,128]{2,1,0:T(8,128)S(1)}, u32[]{:S(2)}, u32[]{:S(2)}) async-start(f32[8,120,128]{2,1,0:T(8,128)} %bitcast.7), calls=%async_computation.3 | async-start | bytes 983040 | tf_op jit(solution)/shard_map/all_to_all | solution.py:355
  59.7 2.9 %orthonormal.1 = (f32[64,64]{1,0:T(8,128)S(1)}, f32[64,1024]{1,0:T(8,128)S(1)}) custom-call(f32[512,128]{1,0:T(8,128)S(1)} %bitcast.15), custom_call_target="tpu_custom_call" | custom-call | flops 40000000 | bytes 600000 | tf_op jit(solution)/shard_map/orthonormal/pallas_call | solution.py:265
  62.6 6.5 %all-to-all-done.3 = f32[8,120,128]{2,1,0:T(8,128)S(1)} async-done(((f32[8,120,128]{2,1,0:T(8,128)}), f32[8,120,128]{2,1,0:T(8,128)S(1)}, u32[]{:S(2)}, u32[]{:S(2)}) %all-to-all-start.3) | async-done | bytes 491552 | tf_op jit(solution)/shard_map/all_to_all | solution.py:355
  69.1 13.1 %all_to_all.31 = f32[4,120,128]{2,1,0:T(8,128)S(1)} all-to-all(f32[4,120,128]{2,1,0:T(8,128)S(1)} %broadcast_in_dim.12), channel_id=1, replica_groups=mesh['x'=4,'zh'=4,'zl'=2,'y'=4,'core'=2] {'zh'}, dimensions={0} | all-to-all | bytes 491520 | tf_op jit(solution)/shard_map/all_to_all | solution.py:355
  82.2 11.7 %all_to_all.32 = f32[8,120,128]{2,1,0:T(8,128)S(1)} all-to-all(f32[8,120,128]{2,1,0:T(8,128)S(1)} %broadcast_in_dim.13), channel_id=1, replica_groups=mesh['x'=4,'zh'=4,'zl'=2,'y'=4,'core'=2] {'x','zl'}, dimensions={0} | all-to-all | bytes 983040 | tf_op jit(solution)/shard_map/all_to_all | solution.py:355
  93.9 3.1 %finish.1 = (f32[64,1024]{1,0:T(8,128)}, bf16[64,1848]{1,0:T(8,128)(2,1)}, bf16[1848,1024]{1,0:T(8,128)(2,1)}) custom-call(f32[960,128]{1,0:T(8,128)S(1)} %bitcast.16, f32[64,64]{1,0:T(8,128)S(1)} %get-tuple-element.18.inverse_ref, f32[64,1024]{1,0:T(8,128)S(1)} %get-tuple-element.19.left_ref, bf16[12288,1024]{1,0:T(8,128)(2,1)} %accumulate.2.acc_a, ...), custom_call_target="tpu_custom_call" | custom-call | flops 242221056 | bytes 8500000 | tf_op jit(solution)/shard_map/finish/pallas_call | solution.py:329
  (7 shorter events, 0.1 us)
Async XLA Ops:
  5.9 16.3 %all-to-all-start = ((f32[32,16,128]{2,1,0:T(8,128)}), f32[32,16,128]{2,1,0:T(8,128)S(1)}, u32[]{:S(2)}, u32[]{:S(2)}) async-start(f32[32,16,128]{2,1,0:T(8,128)} %bitcast.23), calls=%async_computation | async-start | bytes 524288 | tf_op jit(solution)/shard_map/all_to_all | solution.py:355
  38.3 12.8 %all-to-all-start.2 = ((f32[32,16,128]{2,1,0:T(8,128)}), f32[32,16,128]{2,1,0:T(8,128)S(1)}, u32[]{:S(2)}, u32[]{:S(2)}) async-start(f32[32,16,128]{2,1,0:T(8,128)} %broadcast_in_dim.11), calls=%async_computation.2 | async-start | bytes 524288 | tf_op jit(solution)/shard_map/all_to_all | solution.py:355
  42.2 1.5 %copy-start = (bf16[896,1024]{1,0:T(8,128)(2,1)S(1)}, bf16[896,1024]{1,0:T(8,128)(2,1)}, u32[]{:S(2)}) copy-start(bf16[896,1024]{1,0:T(8,128)(2,1)} %act_hbm.5) | copy-start | bytes 5505028
  54.8 14.2 %all-to-all-start.3 = ((f32[8,120,128]{2,1,0:T(8,128)}), f32[8,120,128]{2,1,0:T(8,128)S(1)}, u32[]{:S(2)}, u32[]{:S(2)}) async-start(f32[8,120,128]{2,1,0:T(8,128)} %bitcast.7), calls=%async_computation.3 | async-start | bytes 983040 | tf_op jit(solution)/shard_map/all_to_all | solution.py:355

commit v5 on v4

--- a/solution.py
+++ b/solution.py
@@ -34,14 +34,11 @@
 
 def split(value):
     high = value.astype(jnp.bfloat16)
-    rest = value - high.astype(jnp.float32)
-    middle = rest.astype(jnp.bfloat16)
-    low = (rest - middle.astype(jnp.float32)).astype(jnp.bfloat16)
-    return high, middle, low
+    return high, (value - high.astype(jnp.float32)).astype(jnp.bfloat16)
 
 
 def add_parts(product):
-    return product[:RANK] + (product[RANK : 2 * RANK] + product[2 * RANK :])
+    return product[:RANK] + product[RANK:]
 
 
 def whole_copies(sources, targets, sems):
@@ -103,10 +100,12 @@
     act_ref, grad_ref, error_ref, sems, grad_sems, error_sems, *spare
 ):
     chunks = [(i, a, n) for i, (h, a, n) in enumerate(c for c in CHUNKS if c[0] == half)]
-    act_copy = pltpu.make_async_copy(act_hbm, act_ref, sems.at[0])
+    act_copy = None if half else pltpu.make_async_copy(act_hbm, act_ref, sems.at[0])
+    act_ref = act_hbm if half else act_ref
     grad_copies, error_copies, acc_copies = [], [], []
     acc_ref = spare[0] if spare else out_ref
-    act_copy.start()
+    if act_copy:
+        act_copy.start()
     for i, a, n in chunks:
         here, there = pl.ds(a, n), pl.ds(half * HALF + a, n)
         grad_copies.append(
@@ -119,12 +118,16 @@
             acc_copies.append(
                 pltpu.make_async_copy(acc_ref.at[here], out_ref.at[here], spare[1].at[i])
             )
-        grad_copies[i].start()
-        error_copies[i].start()
-    act_copy.wait()
+    grad_copies[0].start()
+    error_copies[0].start()
+    if act_copy:
+        act_copy.wait()
     for i, a, n in chunks:
         rows = pl.ds(a, n)
         grad_copies[i].wait()
+        if i + 1 < len(chunks):
+            grad_copies[i + 1].start()
+            error_copies[i + 1].start()
         gradient = jnp.dot(grad_ref[rows, :], act_ref[...], preferred_element_type=jnp.float32)
         error_copies[i].wait()
         acc_ref[rows, :] = (error_ref[rows, :].astype(jnp.float32) + gradient).astype(jnp.bfloat16)
@@ -139,11 +142,11 @@
     spare = [pltpu.VMEM((size, ROWS), jnp.bfloat16), pltpu.SemaphoreType.DMA((2,))]
     return pl.pallas_call(
         functools.partial(accumulate_kernel, half),
-        in_specs=[ANY] * 3,
+        in_specs=[WHOLE if half else ANY, ANY, ANY],
         out_specs=WHOLE if half else ANY,
         out_shape=jax.ShapeDtypeStruct((size if half else SPARE_ROWS, ROWS), jnp.bfloat16),
         scratch_shapes=[
-            pltpu.VMEM((TOK, ROWS), jnp.bfloat16),
+            pltpu.VMEM((TOK if half == 0 else 16, ROWS), jnp.bfloat16),
             pltpu.VMEM((size, TOK), jnp.bfloat16),
             pltpu.VMEM((size, ROWS), jnp.bfloat16),
             pltpu.SemaphoreType.DMA((1,)),
@@ -201,13 +204,13 @@
         out_specs=WHOLE,
         out_shape=jax.ShapeDtypeStruct((COL_TILES * RANK, LANES), jnp.float32),
         scratch_shapes=[
-            pltpu.VMEM((3 * RANK, ROWS), jnp.bfloat16),
+            pltpu.VMEM((2 * RANK, ROWS), jnp.bfloat16),
             pltpu.VMEM((HALVES[0], ROWS), jnp.bfloat16),
             pltpu.SemaphoreType.DMA((len(CHUNKS),)),
         ],
         compiler_params=params(),
         cost_estimate=pl.CostEstimate(
-            flops=6 * COLS * ROWS * RANK, bytes_accessed=4_500_000, transcendentals=0
+            flops=4 * COLS * ROWS * RANK, bytes_accessed=4_500_000, transcendentals=0
         ),
         name="project",
     )(left_sum, acc_a, acc_b)

time: 97.6 us -> 97.6 us (level)
  transfers between devices with their start and end apart: 3 -> 3, of which waited for: 3 -> 3; matrix products, arithmetic and copies ran while one was open for 0% -> 0% of each run, Pallas kernels for 13% -> 12%
where the time goes in v5:
time: 97.6 us; the launch traced here: 97 us
  blocking collectives  40.1 us (41%)
  Pallas kernels  23.9 us (24%)
  starting transfers between devices  16.1 us (16%)
  waiting for transfers between devices  13.8 us (14%)
  local copies, waits for them, and re-layouts  2.27 us (2%)
    all_to_all x3, blocking collectives, exchange(): return lax.all_to_all(pieces, axes, 0, 0, tiled=True)  40.1 us
    all_to_all x3, starting transfers between devices, exchange(): return lax.all_to_all(pieces, axes, 0, 0, tiled=True)  16.1 us
    all_to_all x3, waiting for transfers between devices, exchange(): return lax.all_to_all(pieces, axes, 0, 0, tiled=True)  13.8 us
    pallas_call x2, Pallas kernels, accumulate(): pl.pallas_call(functools.partial(accumulate_kernel, half), in_specs=[WHOL...  9.04 us
    pallas_call x1, Pallas kernels, left_term(): pl.pallas_call(left_kernel, in_specs=[ANY] * 4, out_specs=WHOLE, out_shap...  5.29 us
    pallas_call x1, Pallas kernels, project(): pl.pallas_call(project_kernel, in_specs=[WHOLE, ANY, WHOLE], out_specs=WH...  3.63 us
    pallas_call x1, Pallas kernels, finish(): pl.pallas_call(finish_kernel, in_specs=[WHOLE] * 3 + [ANY, WHOLE], out_sp...  3.11 us
    pallas_call x1, Pallas kernels, orthonormal(): pl.pallas_call(orthonormal_kernel, in_specs=[WHOLE], out_specs=[WHOLE, WH...  2.87 us
  transfers between devices with their start and end apart: 3, of which 3 were waited for; matrix products, arithmetic and copies ran while one was open for 0% of the time, Pallas kernels for 12%

profile of v5, /device:TPU:32, one launch (start us, length us, event | category | flops | bytes accessed | tf_op | source)
XLA Modules:
  0.0 97.0 jit_solution(9123569842868685335)
XLA Ops:
  0.6 5.3 %left_term.1 = f32[512,128]{1,0:T(8,128)} custom-call(bf16[896,1024]{1,0:T(8,128)(2,1)} %act_hbm.5, bf16[1848,896]{1,0:T(8,128)(2,1)} %bitcast.20, bf16[1848,1024]{1,0:T(8,128)(2,1)} %bitcast.17, bf16[64,1848]{1,0:T(8,128)(2,1)} %bitcast.24), custom_call_target="tpu_custom_call" | custom-call | flops 571604992 | bytes 9000000 | tf_op jit(solution)/shard_map/left_term/pallas_call | solution.py:77
  5.9 7.3 %all-to-all-start = ((f32[32,16,128]{2,1,0:T(8,128)}), f32[32,16,128]{2,1,0:T(8,128)S(1)}, u32[]{:S(2)}, u32[]{:S(2)}) async-start(f32[32,16,128]{2,1,0:T(8,128)} %bitcast.23), calls=%async_computation | async-start | bytes 524288 | tf_op jit(solution)/shard_map/all_to_all | solution.py:358
  13.3 4.4 %accumulate.2.acc_a = bf16[12288,1024]{1,0:T(8,128)(2,1)} custom-call(bf16[896,1024]{1,0:T(8,128)(2,1)} %act_hbm.5, bf16[1848,896]{1,0:T(8,128)(2,1)} %bitcast.21, bf16[1848,1024]{1,0:T(8,128)(2,1)} %bitcast.18), custom_call_target="tpu_custom_call" | custom-call | flops 1174405120 | bytes 8000000 | tf_op jit(solution)/shard_map/accumulate/pallas_call | solution.py:143
  17.7 4.5 %all-to-all-done = f32[32,16,128]{2,1,0:T(8,128)S(1)} async-done(((f32[32,16,128]{2,1,0:T(8,128)}), f32[32,16,128]{2,1,0:T(8,128)S(1)}, u32[]{:S(2)}, u32[]{:S(2)}) %all-to-all-start) | async-done | bytes 262176 | tf_op jit(solution)/shard_map/all_to_all | solution.py:358
  22.3 15.3 %all_to_all.30 = f32[8,16,128]{2,1,0:T(8,128)S(1)} all-to-all(f32[8,16,128]{2,1,0:T(8,128)S(1)} %broadcast_in_dim.10), channel_id=1, replica_groups=mesh['x'=4,'zh'=4,'zl'=2,'y'=4,'core'=2] {'zh','zl'}, dimensions={0} | all-to-all | bytes 131072 | tf_op jit(solution)/shard_map/all_to_all | solution.py:358
  37.6 0.7 broadcast_in_dim.11
  38.3 3.9 %all-to-all-start.2 = ((f32[32,16,128]{2,1,0:T(8,128)}), f32[32,16,128]{2,1,0:T(8,128)S(1)}, u32[]{:S(2)}, u32[]{:S(2)}) async-start(f32[32,16,128]{2,1,0:T(8,128)} %broadcast_in_dim.11), calls=%async_computation.2 | async-start | bytes 524288 | tf_op jit(solution)/shard_map/all_to_all | solution.py:358
  42.2 0.0 copy-start
  42.2 1.5 %copy-done = bf16[896,1024]{1,0:T(8,128)(2,1)S(1)} copy-done((bf16[896,1024]{1,0:T(8,128)(2,1)S(1)}, bf16[896,1024]{1,0:T(8,128)(2,1)}, u32[]{:S(2)}) %copy-start) | copy-done | bytes 1835032
  43.7 4.6 %accumulate.3.acc_b = bf16[1208,1024]{1,0:T(8,128)(2,1)S(1)} custom-call(bf16[896,1024]{1,0:T(8,128)(2,1)S(1)} %copy-done, bf16[1848,896]{1,0:T(8,128)(2,1)} %bitcast.22, bf16[1848,1024]{1,0:T(8,128)(2,1)} %bitcast.19), custom_call_target="tpu_custom_call" | custom-call | flops 2216689664 | bytes 8000000 | tf_op jit(solution)/shard_map/accumulate/pallas_call | solution.py:143
  48.3 2.8 %all-to-all-done.2 = f32[32,16,128]{2,1,0:T(8,128)S(1)} async-done(((f32[32,16,128]{2,1,0:T(8,128)}), f32[32,16,128]{2,1,0:T(8,128)S(1)}, u32[]{:S(2)}, u32[]{:S(2)}) %all-to-all-start.2) | async-done | bytes 262176 | tf_op jit(solution)/shard_map/all_to_all | solution.py:358
  51.1 3.6 %project.1 = f32[960,128]{1,0:T(8,128)} custom-call(f32[512,128]{1,0:T(8,128)S(1)} %bitcast.14, bf16[12288,1024]{1,0:T(8,128)(2,1)} %accumulate.2.acc_a, bf16[1208,1024]{1,0:T(8,128)(2,1)S(1)} %accumulate.3.acc_b), custom_call_target="tpu_custom_call" | custom-call | flops 484442112 | bytes 4500000 | tf_op jit(solution)/shard_map/project/pallas_call | solution.py:201
  54.7 4.9 %all-to-all-start.3 = ((f32[8,120,128]{2,1,0:T(8,128)}), f32[8,120,128]{2,1,0:T(8,128)S(1)}, u32[]{:S(2)}, u32[]{:S(2)}) async-start(f32[8,120,128]{2,1,0:T(8,128)} %bitcast.7), calls=%async_computation.3 | async-start | bytes 983040 | tf_op jit(solution)/shard_map/all_to_all | solution.py:358
  59.6 2.9 %orthonormal.1 = (f32[64,64]{1,0:T(8,128)S(1)}, f32[64,1024]{1,0:T(8,128)S(1)}) custom-call(f32[512,128]{1,0:T(8,128)S(1)} %bitcast.15), custom_call_target="tpu_custom_call" | custom-call | flops 40000000 | bytes 600000 | tf_op jit(solution)/shard_map/orthonormal/pallas_call | solution.py:268
  62.5 6.5 %all-to-all-done.3 = f32[8,120,128]{2,1,0:T(8,128)S(1)} async-done(((f32[8,120,128]{2,1,0:T(8,128)}), f32[8,120,128]{2,1,0:T(8,128)S(1)}, u32[]{:S(2)}, u32[]{:S(2)}) %all-to-all-start.3) | async-done | bytes 491552 | tf_op jit(solution)/shard_map/all_to_all | solution.py:358
  69.0 13.1 %all_to_all.31 = f32[4,120,128]{2,1,0:T(8,128)S(1)} all-to-all(f32[4,120,128]{2,1,0:T(8,128)S(1)} %broadcast_in_dim.12), channel_id=1, replica_groups=mesh['x'=4,'zh'=4,'zl'=2,'y'=4,'core'=2] {'zh'}, dimensions={0} | all-to-all | bytes 491520 | tf_op jit(solution)/shard_map/all_to_all | solution.py:358
  82.1 11.7 %all_to_all.32 = f32[8,120,128]{2,1,0:T(8,128)S(1)} all-to-all(f32[8,120,128]{2,1,0:T(8,128)S(1)} %broadcast_in_dim.13), channel_id=1, replica_groups=mesh['x'=4,'zh'=4,'zl'=2,'y'=4,'core'=2] {'x','zl'}, dimensions={0} | all-to-all | bytes 983040 | tf_op jit(solution)/shard_map/all_to_all | solution.py:358
  93.9 3.1 %finish.1 = (f32[64,1024]{1,0:T(8,128)}, bf16[64,1848]{1,0:T(8,128)(2,1)}, bf16[1848,1024]{1,0:T(8,128)(2,1)}) custom-call(f32[960,128]{1,0:T(8,128)S(1)} %bitcast.16, f32[64,64]{1,0:T(8,128)S(1)} %get-tuple-element.18.inverse_ref, f32[64,1024]{1,0:T(8,128)S(1)} %get-tuple-element.19.left_ref, bf16[12288,1024]{1,0:T(8,128)(2,1)} %accumulate.2.acc_a, ...), custom_call_target="tpu_custom_call" | custom-call | flops 242221056 | bytes 8500000 | tf_op jit(solution)/shard_map/finish/pallas_call | solution.py:332
  (7 shorter events, 0.1 us)
Async XLA Ops:
  5.9 16.3 %all-to-all-start = ((f32[32,16,128]{2,1,0:T(8,128)}), f32[32,16,128]{2,1,0:T(8,128)S(1)}, u32[]{:S(2)}, u32[]{:S(2)}) async-start(f32[32,16,128]{2,1,0:T(8,128)} %bitcast.23), calls=%async_computation | async-start | bytes 524288 | tf_op jit(solution)/shard_map/all_to_all | solution.py:358
  38.3 12.8 %all-to-all-start.2 = ((f32[32,16,128]{2,1,0:T(8,128)}), f32[32,16,128]{2,1,0:T(8,128)S(1)}, u32[]{:S(2)}, u32[]{:S(2)}) async-start(f32[32,16,128]{2,1,0:T(8,128)} %broadcast_in_dim.11), calls=%async_computation.2 | async-start | bytes 524288 | tf_op jit(solution)/shard_map/all_to_all | solution.py:358
  42.2 1.5 %copy-start = (bf16[896,1024]{1,0:T(8,128)(2,1)S(1)}, bf16[896,1024]{1,0:T(8,128)(2,1)}, u32[]{:S(2)}) copy-start(bf16[896,1024]{1,0:T(8,128)(2,1)} %act_hbm.5) | copy-start | bytes 5505028
  54.7 14.2 %all-to-all-start.3 = ((f32[8,120,128]{2,1,0:T(8,128)}), f32[8,120,128]{2,1,0:T(8,128)S(1)}, u32[]{:S(2)}, u32[]{:S(2)}) async-start(f32[8,120,128]{2,1,0:T(8,128)} %bitcast.7), calls=%async_computation.3 | async-start | bytes 983040 | tf_op jit(solution)/shard_map/all_to_all | solution.py:358
